TPU v7x, 256 devices: a whole 4x4x8 slice. The times are simulated.
256 devices in a mesh: ctx: 32 (over x, z), head: 8 (over y, core).
Axes of the slice: x: 4, y: 4, z: 8, core: 2. Of those that a mesh axis runs over, the one named last changes fastest.
Arguments:
- latents: bfloat16 [2048, 1024], P('ctx'), may hold values from -4 to 4
- frames: bfloat16 [65536, 1024], P(('ctx', 'head')), may hold values from -200 to 200
- block_lists: int32 [16, 256], replicated, may hold values from 0 to 511, as said below
- query_weight: bfloat16 [1024, 1024], P(None, 'head')
- key_weight: bfloat16 [1024, 1024], replicated
- value_weight: bfloat16 [1024, 1024], replicated, may hold values from -0.1875 to 0.1875
- output_weight: bfloat16 [1024, 1024], P('head'), may hold values from -0.1875 to 0.1875
Outputs:
- mixed: bfloat16 [2048, 1024], P(('ctx', 'head'))
Inputs may be any that keep to these rules, and one draw needn't show every extreme that they name: `block_lists`: each row lists 256 different frame blocks in rising order; frame blocks 0 and 511 appear in every row.
All inputs are finite; a program needn't handle non-finite values.
Results may differ from a plain program's by a relative error of at most 0.02.
Values may be sent and summed in bfloat16 or wider, within the bound.
A program may use at most 128 MiB of HBM per device.

v0:
```python
import jax
import jax.numpy as jnp
from jax import lax
from jax.sharding import PartitionSpec as P

HS = 64
BLK = 128


NEG_FILL = -1e30


def merged(value, axis, combine):
    everything = jax.tree.map(lambda part: lax.all_gather(part, axis), value)
    leading = jax.tree.map(lambda part: part[0], everything)

    def hop(k, so_far):
        return combine(so_far, jax.tree.map(lambda part: part[k], everything))

    return lax.fori_loop(1, lax.axis_size(axis), hop, leading)


def combine_pair(first, second):
    first_max, first_total, first_out = first
    second_max, second_total, second_out = second
    top_values = jnp.maximum(first_max, second_max)
    first_factor = jnp.exp(first_max - top_values)
    second_factor = jnp.exp(second_max - top_values)
    merged_total = first_total * first_factor + second_total * second_factor
    merged_out = first_out * jnp.repeat(first_factor, HS, axis=0) + second_out * jnp.repeat(
        second_factor, HS, axis=0
    )
    return (top_values, merged_total, merged_out)


def per_device(latents, frames, block_lists, query_weight, key_weight, value_weight, output_weight):
    scale_factor = HS ** (-0.5)
    local_width = query_weight.shape[1]
    local_heads = local_width // HS
    own_queries = jnp.dot(latents, query_weight, preferred_element_type=jnp.float32).astype(
        jnp.bfloat16
    )
    queries = lax.all_gather(own_queries, "ctx", axis=0, tiled=True)
    key_full = jnp.dot(frames, key_weight, preferred_element_type=jnp.float32).astype(jnp.bfloat16)
    value_full = jnp.dot(frames, value_weight, preferred_element_type=jnp.float32).astype(
        jnp.bfloat16
    )
    key_rows, value_rows = (
        lax.all_to_all(key_full, "head", split_axis=1, concat_axis=0, tiled=True),
        lax.all_to_all(value_full, "head", split_axis=1, concat_axis=0, tiled=True),
    )
    key_count = key_rows.shape[0]
    local_blocks = key_count // BLK
    first_block = lax.axis_index("ctx") * local_blocks
    block_ids = first_block + jnp.arange(local_blocks, dtype=jnp.int32)
    visible = jnp.any(block_lists[:, :, None] == block_ids[None, None, :], axis=1)
    total_rows = queries.shape[0]
    rows_each = min(512, total_rows)
    count_blocks = total_rows // rows_each
    latent_blocks = rows_each // BLK
    query_blocks = queries.reshape(count_blocks, rows_each, local_heads, HS)
    visible_blocks = visible.reshape(count_blocks, latent_blocks, local_blocks)
    key_heads = key_rows.reshape(key_count, local_heads, HS)
    value_heads = value_rows.reshape(key_count, local_heads, HS)

    def attend(operands):
        block_queries, block_visible = operands
        scores = (
            jnp.einsum("qhd,khd->hqk", block_queries, key_heads, preferred_element_type=jnp.float32)
            * scale_factor
        )
        scores = scores.reshape(local_heads, latent_blocks, BLK, local_blocks, BLK)
        allowed = block_visible[None, :, None, :, None]
        scores = jnp.where(allowed, scores, NEG_FILL)
        row_max = jnp.max(scores, axis=(3, 4))
        exponent = jnp.where(allowed, jnp.exp(scores - row_max[:, :, :, None, None]), 0.0)
        row_total = jnp.sum(exponent, axis=(3, 4))
        weights = exponent.astype(jnp.bfloat16).reshape(local_heads, rows_each, key_count)
        partial_value = jnp.einsum(
            "hqk,khd->hdq", weights, value_heads, preferred_element_type=jnp.float32
        )
        return (
            row_max.reshape(local_heads, rows_each),
            row_total.reshape(local_heads, rows_each),
            partial_value,
        )

    block_max, block_total, block_out = lax.map(attend, (query_blocks, visible_blocks))
    maxima = block_max.transpose(1, 0, 2).reshape(local_heads, total_rows)
    totals = block_total.transpose(1, 0, 2).reshape(local_heads, total_rows)
    outputs = block_out.transpose(1, 2, 0, 3).reshape(local_width, total_rows)
    ctx_count = lax.axis_size("ctx")
    own_rows = total_rows // ctx_count
    merged_max, merged_total, merged_out = merged((maxima, totals, outputs), "ctx", combine_pair)
    start_col = lax.axis_index("ctx") * own_rows
    own_total = lax.dynamic_slice_in_dim(merged_total, start_col, own_rows, 1)
    own_out = lax.dynamic_slice_in_dim(merged_out, start_col, own_rows, 1)
    attended = (own_out / jnp.repeat(own_total, HS, axis=0)).T.astype(jnp.bfloat16)
    return lax.psum_scatter(
        jnp.dot(attended, output_weight, preferred_element_type=jnp.float32).astype(jnp.bfloat16),
        "head",
        scatter_dimension=0,
        tiled=True,
    )


def solution(mesh):
    return jax.shard_map(
        per_device,
        mesh=mesh,
        in_specs=(
            P("ctx", None),
            P(("ctx", "head"), None),
            P(),
            P(None, "head"),
            P(),
            P(),
            P("head", None),
        ),
        out_specs=P(("ctx", "head"), None),
        check_vma=False,
    )
```

profile of v0, /device:TPU:1, one launch (start us, length us, event | category | flops | bytes accessed | tf_op | source)
XLA Modules:
  0.0 489.0 jit_solution(5209156562991736685)
XLA Ops:
  8.1 1.8 fusion.22
  10.8 6.6 %all-to-all-start = ((bf16[256,8,128]{2,0,1:T(8,128)(2,1)}), bf16[256,8,128]{2,0,1:T(8,128)(2,1)S(1)}, u32[]{:S(2)}, u32[]{:S(2)}) async-start(bf16[256,8,128]{2,0,1:T(8,128)(2,1)} %bitcast.86), calls=%async_computation | async-start | bytes 1048576 | tf_op jit(solution)/shard_map/all_to_all | solution.py:49
  17.4 2.5 fusion.23
  20.8 6.1 %all-to-all-done = bf16[256,8,128]{2,0,1:T(8,128)(2,1)S(1)} async-done(((bf16[256,8,128]{2,0,1:T(8,128)(2,1)}), bf16[256,8,128]{2,0,1:T(8,128)(2,1)S(1)}, u32[]{:S(2)}, u32[]{:S(2)}) %all-to-all-start) | async-done | bytes 524320 | tf_op jit(solution)/shard_map/all_to_all | solution.py:49
  26.9 4.9 %all-to-all-start.1 = ((bf16[256,8,128]{2,0,1:T(8,128)(2,1)}), bf16[256,8,128]{2,0,1:T(8,128)(2,1)}, u32[]{:S(2)}, u32[]{:S(2)}) async-start(bf16[256,8,128]{2,0,1:T(8,128)(2,1)} %bitcast.85), calls=%async_computation.1 | async-start | bytes 1048576 | tf_op jit(solution)/shard_map/all_to_all | solution.py:50
  32.1 44.7 %all_gather.12 = bf16[2048,128]{1,0:T(8,128)(2,1)} all-gather(bf16[64,128]{1,0:T(8,128)(2,1)S(1)} %convolution_convert_fusion.3), channel_id=1, replica_groups=mesh['ctx'=32,'head'=8] {'ctx'}, dimensions={0}, use_global_device_ids=true | all-gather | bytes 540672 | tf_op jit(solution)/shard_map/all_gather | solution.py:43
  76.7 2.4 reshape.76
  79.2 1.8 copy.36
  85.6 39.2 %while.33 = (s32[]{:T(128)}, f32[4,2,512]{2,1,0:T(2,128)S(1)}, f32[4,2,512]{2,1,0:T(2,128)S(1)}, f32[4,2,64,512]{3,2,1,0:T(8,128)}, pred[4,4,16]{2,1,0:T(4,128)(...) while((s32[]{:T(128)}, f32[4,2,512]{2,1,0:T(2,128)S(1)}, ...), condition=%wide.region_4.5_spmd, body=%wide.region_1.4_spmd.sunk | while | flops 564131840 | bytes 35029328 | solution.py:88
  86.6 2.9 fusion.47
  89.6 2.9 fusion.48
  92.4 3.0 fusion.49
  96.4 2.9 fusion.47
  99.4 2.9 fusion.48
  102.3 3.0 fusion.49
  106.2 2.9 fusion.47
  109.2 2.9 fusion.48
  112.0 3.0 fusion.49
  116.0 2.9 fusion.47
  119.0 2.9 fusion.48
  121.8 3.0 fusion.49
  124.8 1.9 copy.37
  126.7 1.7 all_gather_reshape.11
  128.5 38.9 %all_gather.13 = f32[32,2,2048]{2,1,0:T(2,128)S(1)} all-gather(f32[1,2,2048]{2,1,0:T(2,128)S(1)} %bitcast.118), channel_id=1, replica_groups=mesh['ctx'=32,'head'=8] {'ctx'}, dimensions={0}, use_global_device_ids=true | all-gather | bytes 540672 | tf_op jit(solution)/shard_map/all_gather | solution.py:14
  167.4 38.5 %all_gather.14 = f32[32,2,2048]{2,1,0:T(2,128)S(1)} all-gather(f32[1,2,2048]{2,1,0:T(2,128)S(1)} %bitcast.117), channel_id=1, replica_groups=mesh['ctx'=32,'head'=8] {'ctx'}, dimensions={0}, use_global_device_ids=true | all-gather | bytes 540672 | tf_op jit(solution)/shard_map/all_gather | solution.py:14
  206.7 167.9 %all-gather.2.cloned.1.call-done = f32[32,128,2048]{2,1,0:T(8,128)} async-done(((f32[1,128,2048]{2,1,0:T(8,128)}), f32[32,128,2048]{2,1,0:T(8,128)}) %all-gather.2.cloned.1.call-update) | async-done | bytes 33554448 | tf_op jit(solution)/shard_map/all_gather | solution.py:14
  375.9 77.0 %while.34 = (s32[]{:T(128)}, f32[2,2048]{1,0:T(2,128)S(1)}, f32[2,2048]{1,0:T(2,128)S(1)}, f32[128,2048]{1,0:T(8,128)S(1)}, f32[32,2,2048]{2,1,0:T(2,128)}, /*in...) while((s32[]{:T(128)}, f32[2,2048]{1,0:T(2,128)S(1)}, ...), condition=%wide.region_6.7_spmd, body=%wide.region_5.6_spmd.sunk | while | flops 811013 | bytes 3309711 | solution.py:20
  381.7 1.7 fusion.51
  386.7 1.7 fusion.51
  399.1 1.7 fusion.51
  411.5 1.7 fusion.51
  454.0 28.1 %reduce-scatter.2.cloned.1.call-done = bf16[8,1024]{1,0:T(8,128)(2,1)} async-done(((bf16[64,1024]{1,0:T(8,128)(2,1)}), bf16[8,1024]{1,0:T(8,128)(2,1)}) %reduce-scatter.2.cloned.1.call-update) | async-done | bytes 16400 | tf_op jit(solution)/shard_map/reduce_scatter | solution.py:99
  (121 shorter events, 84.9 us)
Async XLA Ops:
  6.5 1.6 copy-start
  6.5 25.3 %copy-start.5 = (bf16[1024,128]{1,0:T(8,128)(2,1)S(1)}, bf16[1024,128]{1,0:T(8,128)(2,1)}, u32[]{:S(2)}) copy-start(bf16[1024,128]{1,0:T(8,128)(2,1)} %param.14) | copy-start | bytes 786436
  6.5 25.3 %copy-start.7 = (bf16[64,1024]{1,0:T(8,128)(2,1)S(1)}, bf16[64,1024]{1,0:T(8,128)(2,1)}, u32[]{:S(2)}) copy-start(bf16[64,1024]{1,0:T(8,128)(2,1)} %param.11) | copy-start | bytes 393220
  6.5 74.5 %copy-start.8 = (s32[16,256]{1,0:T(8,128)S(1)}, s32[16,256]{1,0:T(8,128)}, u32[]{:S(2)}) copy-start(s32[16,256]{1,0:T(8,128)} %param.13) | copy-start | bytes 49156
  10.8 16.1 %all-to-all-start = ((bf16[256,8,128]{2,0,1:T(8,128)(2,1)}), bf16[256,8,128]{2,0,1:T(8,128)(2,1)S(1)}, u32[]{:S(2)}, u32[]{:S(2)}) async-start(bf16[256,8,128]{2,0,1:T(8,128)(2,1)} %bitcast.86), calls=%async_computation | async-start | bytes 1048576 | tf_op jit(solution)/shard_map/all_to_all | solution.py:49
  26.9 5.1 %copy-start.1 = (bf16[256,8,128]{2,0,1:T(8,128)(2,1)}, bf16[256,8,128]{2,0,1:T(8,128)(2,1)S(1)}, u32[]{:S(2)}) copy-start(bf16[256,8,128]{2,0,1:T(8,128)(2,1)S(1)} %all-to-all-done) | copy-start | bytes 1572868
  26.9 56.2 %all-to-all-start.1 = ((bf16[256,8,128]{2,0,1:T(8,128)(2,1)}), bf16[256,8,128]{2,0,1:T(8,128)(2,1)}, u32[]{:S(2)}, u32[]{:S(2)}) async-start(bf16[256,8,128]{2,0,1:T(8,128)(2,1)} %bitcast.85), calls=%async_computation.1 | async-start | bytes 1048576 | tf_op jit(solution)/shard_map/all_to_all | solution.py:50
  31.8 342.8 %all-gather.2.cloned.1.call-start = ((), (), s32[]{:S(2)}) async-start(), calls=%async_computation.3 | async-start | bytes 34603008 | tf_op jit(solution)/shard_map/all_gather | solution.py:14
  86.6 5.8 %copy-start.4 = (bf16[2048,2,64]{0,2,1:T(8,128)(2,1)S(1)}, bf16[2048,2,64]{0,2,1:T(8,128)(2,1)}, u32[]{:S(2)}) copy-start(bf16[2048,2,64]{0,2,1:T(8,128)(2,1)} %get-tuple-element.442) | copy-start | bytes 1572868 | tf_op jit(solution)/shard_map/while
  96.4 5.8 %copy-start.4 = (bf16[2048,2,64]{0,2,1:T(8,128)(2,1)S(1)}, bf16[2048,2,64]{0,2,1:T(8,128)(2,1)}, u32[]{:S(2)}) copy-start(bf16[2048,2,64]{0,2,1:T(8,128)(2,1)} %get-tuple-element.442) | copy-start | bytes 1572868 | tf_op jit(solution)/shard_map/while
  106.2 5.8 %copy-start.4 = (bf16[2048,2,64]{0,2,1:T(8,128)(2,1)S(1)}, bf16[2048,2,64]{0,2,1:T(8,128)(2,1)}, u32[]{:S(2)}) copy-start(bf16[2048,2,64]{0,2,1:T(8,128)(2,1)} %get-tuple-element.442) | copy-start | bytes 1572868 | tf_op jit(solution)/shard_map/while
  116.0 5.8 %copy-start.4 = (bf16[2048,2,64]{0,2,1:T(8,128)(2,1)S(1)}, bf16[2048,2,64]{0,2,1:T(8,128)(2,1)}, u32[]{:S(2)}) copy-start(bf16[2048,2,64]{0,2,1:T(8,128)(2,1)} %get-tuple-element.442) | copy-start | bytes 1572868 | tf_op jit(solution)/shard_map/while
  128.5 353.6 %reduce-scatter.2.cloned.1.call-start = ((), (), s32[]{:S(2)}) async-start(), calls=%async_computation.4 | async-start | bytes 147456 | tf_op jit(solution)/shard_map/reduce_scatter | solution.py:99
  167.4 38.5 %copy-start.2 = (f32[32,2,2048]{2,1,0:T(2,128)}, f32[32,2,2048]{2,1,0:T(2,128)S(1)}, u32[]{:S(2)}) copy-start(f32[32,2,2048]{2,1,0:T(2,128)S(1)} %all_gather.13) | copy-start | bytes 1572868
  205.9 0.8 copy-start.3
  375.9 77.2 %copy-start.6 = (bf16[128,1024]{1,0:T(8,128)(2,1)S(1)}, bf16[128,1024]{1,0:T(8,128)(2,1)}, u32[]{:S(2)}) copy-start(bf16[128,1024]{1,0:T(8,128)(2,1)} %param.17) | copy-start | bytes 786436
Sparse Core Ops, SparseCore 0:
  128.6 245.9 all-gather.1
  454.1 27.9 reduce-scatter.1
where the time goes:
time: 497 us; the launch traced here: 489 us
  waiting for transfers between devices  202 us (41%)
  blocking collectives  122 us (25%)
  other arithmetic  88.3 us (18%)
  matrix products  29 us (6%)
  local copies, waits for them, and re-layouts  21.5 us (4%)
  between operations  13.6 us (3%)
  starting transfers between devices  11.6 us (2%)
    all_gather x1, waiting for transfers between devices, merged(): everything = jax.tree.map(lambda part: lax.all_gather(part, axis), value)  168 us
    all_gather x2, blocking collectives, merged(): everything = jax.tree.map(lambda part: lax.all_gather(part, axis), value)  77.4 us
    add x31, other arithmetic, combine_pair(): first_out * jnp.repeat(first_factor, HS, axis=0)  51.8 us
    all_gather x1, blocking collectives, per_device(): queries = lax.all_gather(own_queries, 'ctx', axis=0, tiled=True)  44.7 us
    reduce_scatter x1, waiting for transfers between devices, per_device(): lax.psum_scatter(jnp.dot(attended, output_weight, preferred_element_type=...  28.1 us
    add x31, other arithmetic, combine_pair(): merged_total = first_total * first_factor + second_total * second_factor  24.5 us
    dot_general x4, matrix products, attend(): jnp.einsum('hqk,khd->hdq', weights, value_heads, preferred_element_type=j...  12 us
    dot_general x4, matrix products, attend(): jnp.einsum('qhd,khd->hqk', block_queries, key_heads, preferred_element_ty...  11.7 us
  transfers between devices with their start and end apart: 4, of which 3 were waited for; matrix products, arithmetic and copies ran while one was open for 2% of the time, Pallas kernels for 0%

commit v1 on v0

v1 whole, which is shorter than its diff:
```python
import functools

import jax
import jax.numpy as jnp
from jax import lax
from jax.experimental import pallas as pl
from jax.experimental.pallas import tpu as pltpu
from jax.sharding import PartitionSpec as P

HS = 64
BLK = 128
LANES = 2 * HS
PACK = HS + 16
SCALE = HS ** (-0.5) * 1.4426950408889634
NEG = -1e30
MESH = pl.DeviceIdType.MESH
F32, BF16 = jnp.float32, jnp.bfloat16


def near_first(count):
    return sorted(range(count), key=lambda step: (min(step, count - step), step))


def far_first(count):
    return [step for step in near_first(count)[::-1] if step]


def split_parts(value, count):
    parts = []
    for _ in range(count):
        part = value.astype(BF16).astype(F32)
        parts.append(part)
        value = value - part
    return parts


def pack_stats(top, total):
    rows = split_parts(total, 2) + split_parts(top, 3)
    row_id = lax.broadcasted_iota(jnp.int32, (16, top.shape[1]), 0)
    out = jnp.zeros((16, top.shape[1]), F32)
    for index, row in enumerate(rows):
        out = jnp.where(row_id == index, jnp.broadcast_to(row, out.shape), out)
    return out.astype(BF16)


def unpack_stats(stats):
    stats = stats.astype(F32)
    return stats[2:3] + stats[3:4] + stats[4:5], stats[0:1] + stats[1:2]


def kernel(
    nx, nz, ny,
    lat_hbm, fr_hbm, lists_ref, qw_hbm, kw_hbm, vw_hbm, ow_hbm, out_ref,
    lat, fr, qw, kw, vw, ow, bias, q_all, q_aug, kv_send, kv_recv, k_aug, v_aug,
    top_ref, acc, pa_send, pa_recv, pb_send, pb_recv, fin_send, fin_recv,
    load_sem, zq_s, zq_r, xq_s, xq_r, kv_s, kv_r, pa_s, pa_r, pb_s, pb_r, fin_s, fin_r,
):
    ctx, head = lax.axis_index("ctx"), lax.axis_index("head")
    x, z = ctx // nz, lax.rem(ctx, nz)
    y, c = head // 2, lax.rem(head, 2)
    heads = 2 * ny
    own = lat.shape[0]
    group = nz * own
    total_rows = nx * group
    frames = fr.shape[0]
    keys = 2 * frames
    width = out_ref.shape[1]

    loads = []

    def load(src, dst):
        copy = pltpu.make_async_copy(src, dst, load_sem.at[len(loads)])
        copy.start()
        loads.append(copy)
        return copy

    y_order = far_first(ny) + [0]
    load_lat = load(lat_hbm, lat)
    load_qw = load(qw_hbm, qw)
    load_fr = load(fr_hbm, fr)
    load_kv = []
    for i, step in enumerate(y_order):
        cols = pl.ds(pl.multiple_of(lax.rem(y + step, ny) * 2 * LANES, 2 * LANES), 2 * LANES)
        load_kv.append((load(kw_hbm.at[:, cols], kw.at[i]), load(vw_hbm.at[:, cols], vw.at[i])))
    load_ow = load(ow_hbm, ow)

    barrier = pltpu.get_barrier_semaphore()
    z_steps, x_steps, h_steps = far_first(nz), far_first(nx), range(1, heads)

    def z_peer(step):
        return lax.rem(z + step, nz)

    def x_peer(step):
        return lax.rem(x + step, nx)

    def h_peer(step):
        return lax.rem(head + step, heads)

    for step in z_steps:
        pl.semaphore_signal(barrier, inc=1, device_id=(x * nz + z_peer(step), head), device_id_type=MESH)
    for step in x_steps:
        pl.semaphore_signal(barrier, inc=1, device_id=(x_peer(step) * nz + z, head), device_id_type=MESH)
    for step in h_steps:
        pl.semaphore_signal(barrier, inc=1, device_id=(ctx, h_peer(step)), device_id_type=MESH)

    own_rows = pl.ds(pl.multiple_of(ctx * own, own), own)
    load_lat.wait()
    load_qw.wait()
    q_all[own_rows, :] = jnp.dot(lat[...], qw[...], preferred_element_type=F32).astype(BF16)
    pl.semaphore_wait(barrier, len(z_steps) + len(x_steps) + len(h_steps))

    def remote(src, dst, send, recv, device):
        return pltpu.make_async_remote_copy(
            src_ref=src, dst_ref=dst, send_sem=send, recv_sem=recv, device_id=device, device_id_type=MESH
        )

    sent = []

    def push(*args):
        copy = remote(*args)
        copy.start()
        sent.append(copy)

    for step in z_steps:
        push(q_all.at[own_rows, :], q_all.at[own_rows, :], zq_s.at[step], zq_r.at[z], (x * nz + z_peer(step), head))

    load_fr.wait()
    for i, step in enumerate(y_order):
        for copy in load_kv[i]:
            copy.wait()
        yd = lax.rem(y + step, ny)
        k = jnp.dot(fr[...], kw[i], preferred_element_type=F32).astype(BF16)
        v = jnp.dot(fr[...], vw[i], preferred_element_type=F32).astype(BF16)
        for cd in range(2):
            kv_send[i, cd, 0] = k[:, cd * LANES:(cd + 1) * LANES]
            kv_send[i, cd, 1] = v[:, cd * LANES:(cd + 1) * LANES]
        if step:
            for cd in range(2):
                push(kv_send.at[i, cd], kv_recv.at[y, c], kv_s.at[2 * i + cd], kv_r.at[head], (ctx, 2 * yd + cd))
    push(kv_send.at[ny - 1, 1 - c], kv_recv.at[y, c], kv_s.at[2 * ny - 2], kv_r.at[head], (ctx, 2 * y + 1 - c))
    kv_recv[y, c] = kv_send[ny - 1, c]

    lists = lists_ref[...].astype(F32)
    blocks, listed = lists.shape
    unused = jnp.full((HS - blocks, listed), -1.0, F32)
    lists = jnp.concatenate([lists, unused, lists, unused], axis=0).T
    local_blocks = heads * frames // BLK
    for j in range(local_blocks):
        block_id = (ctx * local_blocks + j).astype(F32)
        seen = jnp.max(jnp.where(lists == block_id, 1.0, 0.0), axis=0, keepdims=True)
        bias[j] = jnp.broadcast_to(jnp.where(seen > 0.0, 0.0, NEG), (8, LANES))

    for step in z_steps:
        zs = z_peer(step)
        rows = pl.ds(pl.multiple_of((x * nz + zs) * own, own), own)
        remote(q_all.at[rows, :], q_all.at[rows, :], zq_s.at[step], zq_r.at[zs], (ctx, head)).wait_recv()

    def group_rows(xg):
        return pl.ds(pl.multiple_of(xg * group, group), group)

    for step in x_steps:
        push(
            q_all.at[group_rows(x), :], q_all.at[group_rows(x), :], xq_s.at[step], xq_r.at[x],
            (x_peer(step) * nz + z, head),
        )

    lane = lax.broadcasted_iota(jnp.int32, (1, LANES), 1)
    low = lane < HS

    def build_queries(xg):
        q = q_all[group_rows(xg), :].astype(F32) * SCALE
        high = q.astype(BF16)
        rest = (q - high.astype(F32)).astype(BF16)
        block = (lax.broadcasted_iota(jnp.int32, (group, 1), 0) + xg * group) // BLK
        own_block = jnp.where(lax.rem(lane, HS) == block, 1.0, 0.0).astype(BF16)
        zero = jnp.zeros_like(high)
        for h in range(2):
            mine = low if h == 0 else ~low
            q_aug[h, group_rows(xg), 0:LANES] = jnp.where(mine, high, own_block)
            q_aug[h, group_rows(xg), LANES:2 * LANES] = jnp.where(mine, rest, zero)

    def build_keys(yk):
        vt = []
        for cs in range(2):
            k = kv_recv[yk, cs, 0]
            for j in range(frames // BLK):
                row = bias[(yk * 2 + cs) * (frames // BLK) + j][0:1].astype(BF16)
                place = slice(cs * frames + j * BLK, cs * frames + (j + 1) * BLK)
                kj = k[j * BLK:(j + 1) * BLK]
                for h in range(2):
                    mine = low if h == 0 else ~low
                    k_aug[h, place, 0:LANES] = jnp.where(mine, kj, jnp.broadcast_to(row, kj.shape))
                    k_aug[h, place, LANES:2 * LANES] = kj
            vt.append(kv_recv[yk, cs, 1].astype(F32).T.astype(BF16))
        vt = jnp.concatenate(vt, axis=1)
        ones = jnp.ones((16, keys), BF16)
        for h in range(2):
            v_aug[h, 0:HS] = vt[h * HS:(h + 1) * HS]
            v_aug[h, HS:PACK] = ones

    def attend(rows, first):
        for h in range(2):
            s = lax.dot_general(
                k_aug[h], q_aug[h, rows, :], (((1,), (1,)), ((), ())), preferred_element_type=F32
            )
            top = jnp.max(s, axis=0, keepdims=True)
            if not first:
                old = top_ref[h, 0:1, rows]
                top = jnp.maximum(top, old)
            p = jnp.exp2(s - top).astype(BF16)
            part = jnp.dot(v_aug[h], p, preferred_element_type=F32)
            if not first:
                part = part + acc[h, :, rows] * jnp.exp2(old - top)
            acc[h, :, rows] = part
            top_ref[h, 0:1, rows] = top

    def wait_keys(yk, cores):
        for cs in cores:
            slot = kv_recv.at[yk, cs]
            remote(slot, slot, kv_s.at[0], kv_r.at[2 * yk + cs], (ctx, head)).wait_recv()

    wait_keys(y, [1 - c])
    build_keys(y)
    for step in near_first(nx):
        xg = x_peer(step)
        if step:
            rows = group_rows(xg)
            remote(q_all.at[rows, :], q_all.at[rows, :], xq_s.at[step], xq_r.at[xg], (ctx, head)).wait_recv()
        build_queries(xg)
        attend(group_rows(xg), True)

    others = near_first(ny)[1:]
    for step in others[:-1]:
        yk = lax.rem(y + step, ny)
        wait_keys(yk, range(2))
        build_keys(yk)
        attend(pl.ds(0, total_rows), False)
    yk = lax.rem(y + others[-1], ny)
    wait_keys(yk, range(2))
    build_keys(yk)
    for step in x_steps + [0]:
        xg = x_peer(step)
        rows = group_rows(xg)
        attend(rows, False)
        if step:
            for h in range(2):
                pa_send[step, h, 0:HS] = acc[h, 0:HS, rows].astype(BF16)
                pa_send[step, h, HS:PACK] = pack_stats(top_ref[h, 0:1, rows], acc[h, HS:HS + 1, rows])
            push(pa_send.at[step], pa_recv.at[x], pa_s.at[step], pa_r.at[x], (xg * nz + z, head))

    for step in x_steps:
        slot = pa_recv.at[x_peer(step)]
        remote(slot, slot, pa_s.at[step], pa_r.at[x_peer(step)], (ctx, head)).wait_recv()
    packed = []
    for h in range(2):
        rows = group_rows(x)
        tops, totals = [top_ref[h, 0:1, rows]], [acc[h, HS:HS + 1, rows]]
        for step in x_steps:
            one_top, one_total = unpack_stats(pa_recv[x_peer(step), h, HS:PACK])
            tops.append(one_top)
            totals.append(one_total)
        top = functools.reduce(jnp.maximum, tops)
        factors = [jnp.exp2(one - top) for one in tops]
        total = sum(one * factor for one, factor in zip(totals, factors))
        value = acc[h, 0:HS, rows] * factors[0]
        for step, factor in zip(x_steps, factors[1:]):
            value = value + pa_recv[x_peer(step), h, 0:HS].astype(F32) * factor
        packed.append((value, pack_stats(top, total).astype(F32)))
    for t in range(group // LANES):
        cols = slice(t * LANES, (t + 1) * LANES)
        for part, place in ((0, slice(0, HS)), (1, slice(HS, PACK))):
            a, b = packed[0][part][:, cols], packed[1][part][:, cols]
            pb_send[2 * t, place] = jnp.where(low, a, pltpu.roll(b, HS, 1)).astype(BF16)
            pb_send[2 * t + 1, place] = jnp.where(low, pltpu.roll(a, HS, 1), b).astype(BF16)
    for step in z_steps:
        push(pb_send.at[z_peer(step)], pb_recv.at[z], pb_s.at[step], pb_r.at[z], (x * nz + z_peer(step), head))
    load_ow.wait()

    messages = [pb_send[z]]
    for step in z_steps:
        slot = pb_recv.at[z_peer(step)]
        remote(slot, slot, pb_s.at[step], pb_r.at[z_peer(step)], (ctx, head)).wait_recv()
        messages.append(pb_recv[z_peer(step)])
    stats = [unpack_stats(message[HS:PACK]) for message in messages]
    top = functools.reduce(jnp.maximum, [one for one, _ in stats])
    factors = [jnp.exp2(one - top) for one, _ in stats]
    total = sum(one * factor for (_, one), factor in zip(stats, factors))
    value = sum(message[0:HS].astype(F32) * factor for message, factor in zip(messages, factors))
    attended = (value / total).T.astype(BF16)
    mixed = jnp.dot(attended[0:own], ow[0:HS], preferred_element_type=F32) + jnp.dot(
        attended[own:2 * own], ow[HS:2 * HS], preferred_element_type=F32
    )

    each = own // heads
    half = width // 2
    for h in range(heads):
        rows = mixed[h * each:(h + 1) * each]
        fin_send[h] = jnp.concatenate([rows[:, :half], rows[:, half:]], axis=0).astype(BF16)
    for step in h_steps:
        hd = h_peer(step)
        push(fin_send.at[hd], fin_recv.at[head], fin_s.at[step], fin_r.at[head], (ctx, hd))
    result = fin_send[head].astype(F32)
    for step in h_steps:
        slot = fin_recv.at[h_peer(step)]
        remote(slot, slot, fin_s.at[step], fin_r.at[h_peer(step)], (ctx, head)).wait_recv()
        result = result + fin_recv[h_peer(step)].astype(F32)
    out_ref[:, 0:half] = result[0:each]
    out_ref[:, half:width] = result[each:2 * each]
    for copy in sent:
        copy.wait_send()


def per_device(nx, nz, ny, latents, frames, block_lists, query_weight, key_weight, value_weight, output_weight):
    own, depth = latents.shape
    count = frames.shape[0]
    width = output_weight.shape[1]
    heads, group = 2 * ny, nz * own
    rows = nx * group
    each = own // heads
    any_space, vmem = pl.BlockSpec(memory_space=pl.ANY), pl.BlockSpec(memory_space=pltpu.VMEM)
    dma = pltpu.SemaphoreType.DMA
    mixed = pl.pallas_call(
        functools.partial(kernel, nx, nz, ny),
        out_shape=jax.ShapeDtypeStruct((each, width), F32),
        in_specs=[any_space, any_space, vmem, any_space, any_space, any_space, any_space],
        out_specs=vmem,
        scratch_shapes=[
            pltpu.VMEM((own, depth), BF16),
            pltpu.VMEM((count, depth), BF16),
            pltpu.VMEM((depth, LANES), BF16),
            pltpu.VMEM((ny, depth, 2 * LANES), BF16),
            pltpu.VMEM((ny, depth, 2 * LANES), BF16),
            pltpu.VMEM((LANES, width), BF16),
            pltpu.VMEM((heads * count // BLK, 8, LANES), F32),
            pltpu.VMEM((rows, LANES), BF16),
            pltpu.VMEM((2, rows, 2 * LANES), BF16),
            pltpu.VMEM((ny, 2, 2, count, LANES), BF16),
            pltpu.VMEM((ny, 2, 2, count, LANES), BF16),
            pltpu.VMEM((2, 2 * count, 2 * LANES), BF16),
            pltpu.VMEM((2, PACK, 2 * count), BF16),
            pltpu.VMEM((2, 8, rows), F32),
            pltpu.VMEM((2, PACK, rows), F32),
            pltpu.VMEM((nx, 2, PACK, group), BF16),
            pltpu.VMEM((nx, 2, PACK, group), BF16),
            pltpu.VMEM((nz, PACK, LANES), BF16),
            pltpu.VMEM((nz, PACK, LANES), BF16),
            pltpu.VMEM((heads, 2 * each, width // 2), BF16),
            pltpu.VMEM((heads, 2 * each, width // 2), BF16),
            dma((4 + 2 * ny,)),
            dma((nz,)), dma((nz,)),
            dma((nx,)), dma((nx,)),
            dma((heads,)), dma((heads,)),
            dma((nx,)), dma((nx,)),
            dma((nz,)), dma((nz,)),
            dma((heads,)), dma((heads,)),
        ],
        compiler_params=pltpu.CompilerParams(
            collective_id=0, has_side_effects=True, vmem_limit_bytes=56 * 2**20
        ),
        name="cross_attention",
    )(latents, frames, block_lists, query_weight, key_weight, value_weight, output_weight)
    return mixed.astype(BF16)


def solution(mesh, nx=4, nz=8, ny=4):
    return jax.shard_map(
        functools.partial(per_device, nx, nz, ny),
        mesh=mesh,
        in_specs=(
            P("ctx", None),
            P(("ctx", "head"), None),
            P(),
            P(None, "head"),
            P(),
            P(),
            P("head", None),
        ),
        out_specs=P(("ctx", "head"), None),
        check_vma=False,
    )
```

time: 497 us -> 54.8 us (0.11); the launches traced: 489 us -> 54.6 us
  waiting for transfers between devices: 202 us -> 0 us
  blocking collectives: 122 us -> 0 us
  other arithmetic: 88.3 us -> 1.37 us
  Pallas kernels: 0 us -> 53.2 us
  matrix products: 29 us -> 0 us
  local copies, waits for them, and re-layouts: 21.5 us -> 0 us
  between operations: 13.6 us -> 0.01 us
  starting transfers between devices: 11.6 us -> 0 us
    all_gather x1 -> x0, waiting for transfers between devices: 168 us -> none  [merged(): everything = jax.tree.map(lambda part: lax.all_gather(part, axis), value)]
    all_gather x3 -> x0, blocking collectives: 122 us -> none  [the longest x2 77.4 us: merged(): everything = jax.tree.map(lambda part: lax.all_gather(part, axis), value)]
    add x63 -> x0, other arithmetic: 76.3 us -> none  [the longest x31 51.8 us: combine_pair(): first_out * jnp.repeat(first_factor, HS, axis=0)]
    pallas_call x0 -> x1, Pallas kernels: none -> 53.2 us  [per_device(): pl.pallas_call(functools.partial(kernel, nx, nz, ny), out_shape=jax.Shape...]
    dot_general x12 -> x0, matrix products: 29 us -> none  [the longest x4 12 us: attend(): jnp.einsum('hqk,khd->hdq', weights, value_heads, preferred_element_type=j...]
    reduce_scatter x1 -> x0, waiting for transfers between devices: 28.1 us -> none  [per_device(): lax.psum_scatter(jnp.dot(attended, output_weight, preferred_element_type=...]
    all_to_all x2 -> x0, starting transfers between devices: 11.5 us -> none  [the longest x1 6.63 us: per_device(): lax.all_to_all(key_full, 'head', split_axis=1, concat_axis=0, tiled=True)]
    reduce_sum x4 -> x0, other arithmetic: 11.5 us -> none  [attend(): row_total = jnp.sum(exponent, axis=(3, 4))]
  transfers between devices with their start and end apart: 4 -> 0, of which waited for: 3 -> 0; matrix products, arithmetic and copies ran while one was open for 2% -> 0% of each run, Pallas kernels for 0% -> 0%
where the time goes in v1:
time: 54.8 us; the launch traced here: 54.6 us
  Pallas kernels  53.2 us (97%)
  other arithmetic  1.37 us (2%)
    pallas_call x1, Pallas kernels, per_device(): pl.pallas_call(functools.partial(kernel, nx, nz, ny), out_shape=jax.Shape...  53.2 us
    convert_element_type x1, other arithmetic, per_device(): return mixed.astype(BF16)  1.37 us

profile of v1, /device:TPU:1, one launch (start us, length us, event | category | flops | bytes accessed | tf_op | source)
XLA Modules:
  0.0 54.6 jit_solution(9154441144518362066)
XLA Ops:
  0.0 53.2 %cross_attention.1 = f32[8,1024]{1,0:T(8,128)} custom-call(bf16[64,1024]{1,0:T(8,128)(2,1)} %lat_hbm.1, bf16[256,1024]{1,0:T(8,128)(2,1)} %fr_hbm.1, s32[16,256]{1,0:T(8,128)} %lists_ref.1, bf16[1024,128]{1,0:T(8,128)(2,1)} %qw_hbm.1, bf16[1024,1024]{1,0:T(8,128)(2,1)} %kw_hbm.1, bf16[1024,1024]{1,0:T(8,128)(2,1)} %vw_hbm.1, bf16[128,1024]{1,0:T(8,128)(2,1)} %ow_hbm.1), custom_call_target="tpu_custom_call" | custom-call | tf_op jit(solution)/shard_map/cross_attention/pallas_call | solution.py:322
  53.2 1.4 %convert_element_type.3 = bf16[8,1024]{1,0:T(8,128)(2,1)} convert(f32[8,1024]{1,0:T(8,128)} %cross_attention.1) | non-fusion elementwise | flops 8192 | bytes 49152 | tf_op jit(solution)/shard_map/convert_element_type | solution.py:362

commit v2 on v1

v2 whole, which is shorter than its diff:
```python
import functools

import jax
import jax.numpy as jnp
from jax import lax
from jax.experimental import pallas as pl
from jax.experimental.pallas import tpu as pltpu
from jax.sharding import PartitionSpec as P

HS = 64
BLK = 128
LANES = 2 * HS
PACK = HS + 16
SCALE = HS ** (-0.5) * 1.4426950408889634
NEG = -1e30
MESH = pl.DeviceIdType.MESH
F32, BF16 = jnp.float32, jnp.bfloat16


def near_first(count):
    return sorted(range(count), key=lambda step: (min(step, count - step), step))


def far_first(count):
    return [step for step in near_first(count)[::-1] if step]


def split_parts(value, count):
    parts = []
    for _ in range(count):
        part = value.astype(BF16).astype(F32)
        parts.append(part)
        value = value - part
    return parts


def pack_stats(top, total):
    rows = split_parts(total, 2) + split_parts(top, 3)
    row_id = lax.broadcasted_iota(jnp.int32, (16, top.shape[1]), 0)
    out = jnp.zeros((16, top.shape[1]), F32)
    for index, row in enumerate(rows):
        out = jnp.where(row_id == index, jnp.broadcast_to(row, out.shape), out)
    return out.astype(BF16)


def unpack_stats(stats):
    stats = stats.astype(F32)
    return stats[2:3] + stats[3:4] + stats[4:5], stats[0:1] + stats[1:2]


def kernel(
    nx, nz, ny,
    lat_hbm, fr_hbm, lists_ref, qw_hbm, kw_hbm, vw_hbm, ow_hbm, out_ref,
    lat, fr, qw, kw, vw, ow, bias, q_own, q_recv, q_aug, kv_send, kv_recv, k_aug, v_aug,
    scores_0, scores_1, top_ref, acc, p_send, p_recv, fin_send, fin_recv,
    load_sem, q_s, q_r, kv_s, kv_r, p_s, p_r, fin_s, fin_r,
):
    ctx, head = lax.axis_index("ctx"), lax.axis_index("head")
    x, z = ctx // nz, lax.rem(ctx, nz)
    y, c = head // 2, lax.rem(head, 2)
    heads = 2 * ny
    own = lat.shape[0]
    group = nz * own
    width = out_ref.shape[1]
    quarter = lax.rem(x + y, ny)

    def up(value, step, count):
        return lax.rem(value + step, count)

    def down(value, step, count):
        return lax.rem(value + count - step, count)

    loads = []

    def load(src, dst):
        copy = pltpu.make_async_copy(src, dst, load_sem.at[len(loads)])
        copy.start()
        loads.append(copy)
        return copy

    y_order = far_first(ny) + [0]
    load_lat = load(lat_hbm, lat)
    load_qw = load(qw_hbm, qw)
    load_fr = load(fr_hbm, fr)
    load_kv = []
    for step in y_order:
        cols = pl.ds(pl.multiple_of(up(quarter, step, ny) * 2 * LANES, 2 * LANES), 2 * LANES)
        load_kv.append((load(kw_hbm.at[:, cols], kw.at[step]), load(vw_hbm.at[:, cols], vw.at[step])))
    load_ow = load(ow_hbm, ow)

    def user(dx, dz):
        xt = up(x, dx, nx)
        return (xt * nz + up(z, dz, nz), 2 * down(y, xt, ny) + c)

    def owner(dx, dz):
        return (down(x, dx, nx) * nz + down(z, dz, nz), 2 * quarter + c)

    def other_device(dx, dz, action):
        if dx or dz:
            action()
        else:
            pl.when(x != 0)(action)

    x_order = range(nx)
    z_order = far_first(nz) + [0]
    ways = [(dx, dz) for dx in x_order for dz in z_order]

    barrier = pltpu.get_barrier_semaphore()

    def greet(device):
        pl.semaphore_signal(barrier, inc=1, device_id=device, device_id_type=MESH)

    for dx, dz in ways:
        other_device(dx, dz, lambda: greet(owner(dx, dz)))
    for f in range(2):
        for step in range(1, ny):
            core = c if f == 0 else 1 - c
            greet((ctx, 2 * down(y, step, ny) + core))
            greet((down(x, step, nx) * nz + z, 2 * y + core))
    greet((ctx, 2 * y + 1 - c))

    load_lat.wait()
    load_qw.wait()
    q_own[...] = (jnp.dot(lat[...], qw[...], preferred_element_type=F32) * SCALE).astype(BF16)
    pl.semaphore_wait(barrier, nx * nz + 4 * (ny - 1) + jnp.minimum(x, 1))

    def remote(src, dst, send, recv, device):
        return pltpu.make_async_remote_copy(
            src_ref=src, dst_ref=dst, send_sem=send, recv_sem=recv, device_id=device, device_id_type=MESH
        )

    sent = []

    def push(*args):
        copy = remote(*args)
        copy.start()
        sent.append(copy)

    def q_copy(dx, dz):
        index = dx * nz + dz
        return remote(q_own, q_recv.at[dx, dz], q_s.at[index], q_r.at[index], user(dx, dz))

    for dx, dz in ways:
        other_device(dx, dz, lambda: q_copy(dx, dz).start())

    @pl.when(x == 0)
    def _():
        q_recv[0, 0] = q_own[...]

    load_fr.wait()
    for i, step in enumerate(y_order):
        for copy in load_kv[i]:
            copy.wait()
        for part, weight in ((0, kw), (1, vw)):
            rows = jnp.dot(fr[...], weight[step], preferred_element_type=F32).astype(BF16)
            for block in range(2):
                for cd in range(2):
                    kv_send[step, block, cd, part] = rows[
                        block * BLK:(block + 1) * BLK, cd * LANES:(cd + 1) * LANES
                    ]
        for f in range(2):
            core = c if f == 0 else 1 - c
            for block in range(2):
                index = (step * 2 + block) * 2 + f
                if step:
                    if block == 0:
                        device = (ctx, 2 * up(y, step, ny) + core)
                    else:
                        device = (up(x, step, nx) * nz + z, 2 * y + core)
                elif f:
                    device = (ctx, 2 * y + core)
                else:
                    kv_recv[0, block, 0] = kv_send[0, block, core]
                    continue
                push(
                    kv_send.at[step, block, core], kv_recv.at[step, block, f],
                    kv_s.at[index], kv_r.at[index], device,
                )

    lists = lists_ref[...].astype(F32)
    blocks, listed = lists.shape
    unused = jnp.full((HS - blocks, listed), -1.0, F32)
    lists = jnp.concatenate([lists, unused, lists, unused], axis=0).T
    for step in range(ny):
        for block in range(2):
            for f in range(2):
                core = c if f == 0 else 1 - c
                if block == 0:
                    first = ctx * heads + 2 * down(y, step, ny) + core
                else:
                    first = (down(x, step, nx) * nz + z) * heads + 2 * y + core
                block_id = (first * 2 + block).astype(F32)
                seen = jnp.max(jnp.where(lists == block_id, 1.0, 0.0), axis=0, keepdims=True)
                bias[step, block, f] = jnp.broadcast_to(jnp.where(seen > 0.0, 0.0, NEG), (8, LANES))

    lane = lax.broadcasted_iota(jnp.int32, (1, LANES), 1)
    low = lane < HS

    def build_queries(dx):
        for dz in z_order:
            index = dx * nz + dz
            slot = q_recv.at[dx, dz]
            other_device(
                dx, dz,
                lambda: remote(slot, slot, q_s.at[index], q_r.at[index], (ctx, head)).wait_recv(),
            )
        for dz in range(nz):
            q = q_recv[dx, dz]
            block = (down(x, dx, nx) * nz + down(z, dz, nz)) * own // BLK
            own_block = jnp.where(lax.rem(lane, HS) == block, 1.0, 0.0).astype(BF16)
            own_block = jnp.broadcast_to(own_block, q.shape)
            rows = slice(dx * group + dz * own, dx * group + (dz + 1) * own)
            q_aug[0, rows] = jnp.where(low, q, own_block)
            q_aug[1, rows] = jnp.where(low, own_block, q)

    def build_keys(step):
        for block in range(2):
            for f in range(2):
                index = (step * 2 + block) * 2 + f
                slot = kv_recv.at[step, block, f]
                if step or f:
                    remote(slot, slot, kv_s.at[index], kv_r.at[index], (ctx, head)).wait_recv()
        for block in range(2):
            for f in range(2):
                index = (step * 2 + block) * 2 + f
                place = slice(index * BLK, (index + 1) * BLK)
                k = kv_recv[step, block, f, 0]
                hidden = jnp.broadcast_to(bias[step, block, f][0:1].astype(BF16), k.shape)
                k_aug[0, place] = jnp.where(low, k, hidden)
                k_aug[1, place] = jnp.where(low, hidden, k)
                v = kv_recv[step, block, f, 1].astype(F32).T.astype(BF16)
                for h in range(2):
                    v_aug[h, 0:HS, place] = v[h * HS:(h + 1) * HS]
                    v_aug[h, HS:PACK, place] = jnp.ones((PACK - HS, BLK), BF16)

    def product(keys, queries):
        return lax.dot_general(keys, queries, (((1,), (1,)), ((), ())), preferred_element_type=F32)

    def send_partials(dx, values, tops):
        packed = []
        for value, top in zip(values, tops):
            packed.append((value[0:HS], pack_stats(top, value[HS:HS + 1]).astype(F32)))
        for t in range(group // LANES):
            cols = slice(t * LANES, (t + 1) * LANES)
            for part, place in ((0, slice(0, HS)), (1, slice(HS, PACK))):
                a, b = packed[0][part][:, cols], packed[1][part][:, cols]
                p_send[dx, 2 * t, place] = jnp.where(low, a, pltpu.roll(b, HS, 1)).astype(BF16)
                p_send[dx, 2 * t + 1, place] = jnp.where(low, pltpu.roll(a, HS, 1), b).astype(BF16)
        for dz in z_order:
            other_device(dx, dz, lambda: p_copy(dx, dz).start())
        if dx == 0:

            @pl.when(x == 0)
            def _():
                p_recv[0, 0] = p_send[0, 0]

    def p_copy(dx, dz):
        index = dx * nz + dz
        return remote(p_send.at[dx, dz], p_recv.at[dx, dz], p_s.at[index], p_r.at[index], owner(dx, dz))

    build_queries(0)
    rows = slice(0, group)
    for step in range(ny):
        build_keys(step)
        keys = slice(step * 4 * BLK, (step + 1) * 4 * BLK)
        for h in range(2):
            s = product(k_aug[h, keys], q_aug[h, rows])
            top = jnp.max(s, axis=0, keepdims=True)
            if step:
                old = top_ref[h, 0:1]
                top = jnp.maximum(top, old)
            part = jnp.dot(v_aug[h, :, keys], jnp.exp2(s - top).astype(BF16), preferred_element_type=F32)
            if step:
                part = part + acc[h] * jnp.exp2(old - top)
            acc[h] = part
            top_ref[h, 0:1] = top
    send_partials(0, [acc[0], acc[1]], [top_ref[0, 0:1], top_ref[1, 0:1]])

    for dx in x_order[1:]:
        build_queries(dx)
    units = [(dx, h) for dx in x_order[1:] for h in range(2)]
    buffers = (scores_0, scores_1)

    def score(u):
        dx, h = units[u]
        s = product(k_aug[h], q_aug[h, dx * group:(dx + 1) * group])
        buffers[u % 2][...] = s
        return jnp.max(s, axis=0, keepdims=True)

    top = score(0)
    done = []
    for u, (dx, h) in enumerate(units):
        later = score(u + 1) if u + 1 < len(units) else None
        weights = jnp.exp2(buffers[u % 2][...] - top).astype(BF16)
        done.append((jnp.dot(v_aug[h], weights, preferred_element_type=F32), top))
        if h == 1:
            send_partials(dx, [one for one, _ in done], [one for _, one in done])
            done = []
        top = later

    top = total = value = None
    for dx in x_order:
        for dz in z_order:
            index = dx * nz + dz
            slot = p_recv.at[dx, dz]
            other_device(
                dx, dz,
                lambda: remote(slot, slot, p_s.at[index], p_r.at[index], (ctx, head)).wait_recv(),
            )
        stats = [unpack_stats(p_recv[dx, dz, HS:PACK]) for dz in range(nz)]
        tops = [one for one, _ in stats] + ([] if top is None else [top])
        new_top = functools.reduce(jnp.maximum, tops)
        if top is not None:
            factor = jnp.exp2(top - new_top)
            total, value = total * factor, value * factor
        for dz, (one_top, one_total) in enumerate(stats):
            factor = jnp.exp2(one_top - new_top)
            one_total = one_total * factor
            one_value = p_recv[dx, dz, 0:HS].astype(F32) * factor
            total = one_total if total is None else total + one_total
            value = one_value if value is None else value + one_value
        top = new_top
    load_ow.wait()
    attended = (value / total).T.astype(BF16)
    mixed = jnp.dot(attended[0:own], ow[0:HS], preferred_element_type=F32) + jnp.dot(
        attended[own:2 * own], ow[HS:2 * HS], preferred_element_type=F32
    )

    each = own // heads
    half = width // 2
    for h in range(heads):
        rows = mixed[h * each:(h + 1) * each]
        fin_send[h] = jnp.concatenate([rows[:, :half], rows[:, half:]], axis=0).astype(BF16)
    h_steps = range(1, heads)
    for step in h_steps:
        hd = up(head, step, heads)
        push(fin_send.at[hd], fin_recv.at[step], fin_s.at[step], fin_r.at[step], (ctx, hd))
    result = fin_send[head].astype(F32)
    for step in h_steps:
        slot = fin_recv.at[step]
        remote(slot, slot, fin_s.at[step], fin_r.at[step], (ctx, head)).wait_recv()
        result = result + fin_recv[step].astype(F32)
    out_ref[...] = jnp.concatenate([result[0:each], result[each:2 * each]], axis=1).astype(out_ref.dtype)
    for copy in sent:
        copy.wait_send()
    for dx, dz in ways:
        other_device(dx, dz, lambda: q_copy(dx, dz).wait_send())
        other_device(dx, dz, lambda: p_copy(dx, dz).wait_send())


def per_device(nx, nz, ny, latents, frames, block_lists, query_weight, key_weight, value_weight, output_weight):
    own, depth = latents.shape
    count = frames.shape[0]
    width = output_weight.shape[1]
    heads, group = 2 * ny, nz * own
    rows = nx * group
    keys = ny * 4 * BLK
    each = own // heads
    any_space, vmem = pl.BlockSpec(memory_space=pl.ANY), pl.BlockSpec(memory_space=pltpu.VMEM)
    dma = pltpu.SemaphoreType.DMA
    return pl.pallas_call(
        functools.partial(kernel, nx, nz, ny),
        out_shape=jax.ShapeDtypeStruct((each, width), BF16),
        in_specs=[any_space, any_space, vmem, any_space, any_space, any_space, any_space],
        out_specs=vmem,
        scratch_shapes=[
            pltpu.VMEM((own, depth), BF16),
            pltpu.VMEM((count, depth), BF16),
            pltpu.VMEM((depth, LANES), BF16),
            pltpu.VMEM((ny, depth, 2 * LANES), BF16),
            pltpu.VMEM((ny, depth, 2 * LANES), BF16),
            pltpu.VMEM((LANES, width), BF16),
            pltpu.VMEM((ny, 2, 2, 8, LANES), F32),
            pltpu.VMEM((own, LANES), BF16),
            pltpu.VMEM((nx, nz, own, LANES), BF16),
            pltpu.VMEM((2, rows, LANES), BF16),
            pltpu.VMEM((ny, 2, 2, 2, BLK, LANES), BF16),
            pltpu.VMEM((ny, 2, 2, 2, BLK, LANES), BF16),
            pltpu.VMEM((2, keys, LANES), BF16),
            pltpu.VMEM((2, PACK, keys), BF16),
            pltpu.VMEM((keys, group), F32),
            pltpu.VMEM((keys, group), F32),
            pltpu.VMEM((2, 8, group), F32),
            pltpu.VMEM((2, PACK, group), F32),
            pltpu.VMEM((nx, nz, PACK, LANES), BF16),
            pltpu.VMEM((nx, nz, PACK, LANES), BF16),
            pltpu.VMEM((heads, 2 * each, width // 2), BF16),
            pltpu.VMEM((heads, 2 * each, width // 2), BF16),
            dma((4 + 2 * ny,)),
            dma((nx * nz,)), dma((nx * nz,)),
            dma((4 * ny,)), dma((4 * ny,)),
            dma((nx * nz,)), dma((nx * nz,)),
            dma((heads,)), dma((heads,)),
        ],
        compiler_params=pltpu.CompilerParams(
            collective_id=0, has_side_effects=True, vmem_limit_bytes=56 * 2**20
        ),
        name="cross_attention",
    )(latents, frames, block_lists, query_weight, key_weight, value_weight, output_weight)


def solution(mesh, nx=4, nz=8, ny=4):
    return jax.shard_map(
        functools.partial(per_device, nx, nz, ny),
        mesh=mesh,
        in_specs=(
            P("ctx", None),
            P(("ctx", "head"), None),
            P(),
            P(None, "head"),
            P(),
            P(),
            P("head", None),
        ),
        out_specs=P(("ctx", "head"), None),
        check_vma=False,
    )
```

time: 54.8 us -> 62 us (1.13)
  Pallas kernels: 53.2 us -> 60.4 us
  other arithmetic: 1.37 us -> 0 us
  local copies, waits for them, and re-layouts: 0 us -> 1.32 us
    pallas_call x1, Pallas kernels: 53.2 us -> 60.4 us  [per_device(): pl.pallas_call(functools.partial(kernel, nx, nz, ny), out_shape=jax.Shape...]
    convert_element_type x1 -> x0, other arithmetic: 1.37 us -> none  [per_device(): return mixed.astype(BF16)]
    unnamed x0 -> x1, local copies, waits for them, and re-layouts: none -> 1.32 us
where the time goes in v2:
time: 62 us; the launch traced here: 61.7 us
  Pallas kernels  60.4 us (97%)
  local copies, waits for them, and re-layouts  1.32 us (2%)
    pallas_call x1, Pallas kernels, per_device(): pl.pallas_call(functools.partial(kernel, nx, nz, ny), out_shape=jax.Shape...  60.4 us
    unnamed x1, local copies, waits for them, and re-layouts  1.32 us

profile of v2, /device:TPU:1, one launch (start us, length us, event | category | flops | bytes accessed | tf_op | source)
XLA Modules:
  0.0 61.7 jit_solution(18042291613774733914)
XLA Ops:
  0.0 60.4 %cross_attention.1 = bf16[8,1024]{1,0:T(8,128)(2,1)} custom-call(bf16[64,1024]{1,0:T(8,128)(2,1)} %lat_hbm.1, bf16[256,1024]{1,0:T(8,128)(2,1)} %fr_hbm.1, s32[16,256]{1,0:T(8,128)} %lists_ref.1, bf16[1024,128]{1,0:T(8,128)(2,1)} %qw_hbm.1, bf16[1024,1024]{1,0:T(8,128)(2,1)} %kw_hbm.1, bf16[1024,1024]{1,0:T(8,128)(2,1)} %vw_hbm.1, bf16[128,1024]{1,0:T(8,128)(2,1)} %ow_hbm.1), custom_call_target="tpu_custom_call" | custom-call | tf_op jit(solution)/shard_map/cross_attention/pallas_call | solution.py:361
  60.4 1.3 %copy.9 = bf16[8,1024]{1,0:T(8,128)(2,1)} copy(bf16[8,1024]{1,0:T(8,128)(2,1)} %cross_attention.1) | data formatting | bytes 32768

commit v3 on v2

v3 whole, which is shorter than its diff:
```python
import functools

import jax
import jax.numpy as jnp
from jax import lax
from jax.experimental import pallas as pl
from jax.experimental.pallas import tpu as pltpu
from jax.sharding import PartitionSpec as P

HS = 64
BLK = 128
LANES = 2 * HS
PACK = HS + 16
SCALE = HS ** (-0.5) * 1.4426950408889634
NEG = -1e30
MESH = pl.DeviceIdType.MESH
F32, BF16 = jnp.float32, jnp.bfloat16


def near_first(count):
    return sorted(range(count), key=lambda step: (min(step, count - step), step))


def far_first(count):
    return [step for step in near_first(count)[::-1] if step]


def split_parts(value, count):
    parts = []
    for _ in range(count):
        part = value.astype(BF16).astype(F32)
        parts.append(part)
        value = value - part
    return parts


def pack_stats(top, total):
    rows = split_parts(total, 2) + split_parts(top, 3)
    row_id = lax.broadcasted_iota(jnp.int32, (16, top.shape[1]), 0)
    out = jnp.zeros((16, top.shape[1]), F32)
    for index, row in enumerate(rows):
        out = jnp.where(row_id == index, jnp.broadcast_to(row, out.shape), out)
    return out.astype(BF16)


def unpack_stats(stats):
    stats = stats.astype(F32)
    return stats[2:3] + stats[3:4] + stats[4:5], stats[0:1] + stats[1:2]


def kernel(
    nx, nz, ny,
    lat_hbm, fr_hbm, lists_hbm, qw_hbm, kw_hbm, vw_hbm, ow_hbm, out_ref,
    lat, fr, lists_ref, qw, kw, vw, ow, bias, q_own, q_recv, q_aug, kv_send, kv_recv, k_aug, v_aug,
    scores_0, scores_1, top_ref, acc, a_send, a_recv, p_send, p_recv, fin_send, fin_recv,
    load_sem, q_s, q_r, qx_s, qx_r, kv_s, kv_r, a_s, a_r, p_s, p_r, fin_s, fin_r,
):
    ctx, head = lax.axis_index("ctx"), lax.axis_index("head")
    x, z = ctx // nz, lax.rem(ctx, nz)
    y, c = head // 2, lax.rem(head, 2)
    heads = 2 * ny
    own = lat.shape[0]
    group = nz * own
    width = out_ref.shape[1]
    quarter = lax.rem(y + z, ny)
    at_home = lax.rem(z, ny) == 0

    def up(value, step, count):
        return lax.rem(value + step, count)

    def down(value, step, count):
        return lax.rem(value + count - step, count)

    loads = []

    def load(src, dst):
        copy = pltpu.make_async_copy(src, dst, load_sem.at[len(loads)])
        copy.start()
        loads.append(copy)
        return copy

    y_order = far_first(ny) + [0]
    load_lat = load(lat_hbm, lat)
    load_qw = load(qw_hbm, qw)
    load_lists = load(lists_hbm, lists_ref)
    load_fr = load(fr_hbm, fr)
    load_kv = []
    for step in y_order:
        cols = pl.ds(pl.multiple_of(up(quarter, step, ny) * 2 * LANES, 2 * LANES), 2 * LANES)
        load_kv.append((load(kw_hbm.at[:, cols], kw.at[step]), load(vw_hbm.at[:, cols], vw.at[step])))
    load_ow = load(ow_hbm, ow)

    def user(dz):
        zt = up(z, dz, nz)
        return (x * nz + zt, 2 * down(y, lax.rem(zt, ny), ny) + c)

    def owner(dz):
        return (x * nz + down(z, dz, nz), 2 * quarter + c)

    def other_device(dz, action):
        if dz:
            action()
        else:
            pl.when(jnp.logical_not(at_home))(action)

    def z_steps(step, core):
        if step in (0, 1):
            return step
        if step == ny - 1:
            return nz - 1
        return step + core * (nz - 2 * step)

    def core_of(f):
        return c if f == 0 else 1 - c

    def frames_to(step, block, f):
        if block == 0:
            return (ctx, 2 * up(y, step, ny) + core_of(f))
        return (x * nz + up(z, z_steps(step, c), nz), 2 * y + core_of(f))

    def frames_from(step, block, f):
        if block == 0:
            return (ctx, 2 * down(y, step, ny) + core_of(f))
        return (x * nz + down(z, z_steps(step, core_of(f)), nz), 2 * y + core_of(f))

    barrier = pltpu.get_barrier_semaphore()

    def greet(device):
        pl.semaphore_signal(barrier, inc=1, device_id=device, device_id_type=MESH)

    z_far, x_far = far_first(nz), far_first(nx)
    for dz in z_far + [0]:
        other_device(dz, lambda: greet(owner(dz)))
    for dx in x_far:
        greet((down(x, dx, nx) * nz + z, head))
    for step in far_first(ny):
        for block in range(2):
            for f in range(2):
                greet(frames_from(step, block, f))
    greet((ctx, 2 * y + 1 - c))

    load_lat.wait()
    load_qw.wait()
    q_own[...] = (jnp.dot(lat[...], qw[...], preferred_element_type=F32) * SCALE).astype(BF16)
    greeted = nz - 1 + nx - 1 + 4 * (ny - 1) + 1
    pl.semaphore_wait(barrier, greeted + jnp.minimum(lax.rem(z, ny), 1))

    def remote(src, dst, send, recv, device):
        return pltpu.make_async_remote_copy(
            src_ref=src, dst_ref=dst, send_sem=send, recv_sem=recv, device_id=device, device_id_type=MESH
        )

    sent = []

    def push(*args):
        copy = remote(*args)
        copy.start()
        sent.append(copy)

    def q_copy(dz):
        return remote(q_own, q_recv.at[0, dz], q_s.at[dz], q_r.at[dz], user(dz))

    for dz in z_far + [0]:
        other_device(dz, lambda: q_copy(dz).start())

    @pl.when(at_home)
    def _():
        q_recv[0, 0] = q_own[...]

    load_lists.wait()
    lists = lists_ref[...].astype(F32)
    blocks, listed = lists.shape
    unused = jnp.full((HS - blocks, listed), -1.0, F32)
    lists = jnp.concatenate([lists, unused, lists, unused], axis=0).T
    for step in range(ny):
        for block in range(2):
            for f in range(2):
                from_ctx, from_head = frames_from(step, block, f)
                block_id = ((from_ctx * heads + from_head) * 2 + block).astype(F32)
                seen = jnp.max(jnp.where(lists == block_id, 1.0, 0.0), axis=0, keepdims=True)
                bias[step, block, f] = jnp.broadcast_to(jnp.where(seen > 0.0, 0.0, NEG), (8, LANES))

    load_fr.wait()
    for i, step in enumerate(y_order):
        for copy in load_kv[i]:
            copy.wait()
        for part, weight in ((0, kw), (1, vw)):
            rows = jnp.dot(fr[...], weight[step], preferred_element_type=F32).astype(BF16)
            for block in range(2):
                for cd in range(2):
                    kv_send[step, block, cd, part] = rows[
                        block * BLK:(block + 1) * BLK, cd * LANES:(cd + 1) * LANES
                    ]
        for f in range(2):
            for block in range(2):
                index = (step * 2 + block) * 2 + f
                if step or f:
                    push(
                        kv_send.at[step, block, core_of(f)], kv_recv.at[step, block, f],
                        kv_s.at[index], kv_r.at[index], frames_to(step, block, f),
                    )
                else:
                    kv_recv[0, block, 0] = kv_send[0, block, c]

    for dz in near_first(nz):
        slot = q_recv.at[0, dz]
        other_device(dz, lambda: remote(slot, slot, q_s.at[dz], q_r.at[dz], (ctx, head)).wait_recv())
        for dx in x_far:
            index = dx * nz + dz
            push(slot, q_recv.at[dx, dz], qx_s.at[index], qx_r.at[index], (up(x, dx, nx) * nz + z, head))

    lane = lax.broadcasted_iota(jnp.int32, (1, LANES), 1)
    low = lane < HS

    def build_queries(dx):
        if dx:
            for dz in range(nz):
                index = dx * nz + dz
                slot = q_recv.at[dx, dz]
                remote(slot, slot, qx_s.at[index], qx_r.at[index], (ctx, head)).wait_recv()
        for dz in range(nz):
            q = q_recv[dx, dz]
            block = (down(x, dx, nx) * nz + down(z, dz, nz)) * own // BLK
            own_block = jnp.where(lax.rem(lane, HS) == block, 1.0, 0.0).astype(BF16)
            own_block = jnp.broadcast_to(own_block, q.shape)
            rows = slice(dx * group + dz * own, dx * group + (dz + 1) * own)
            q_aug[0, rows] = jnp.where(low, q, own_block)
            q_aug[1, rows] = jnp.where(low, own_block, q)

    def build_keys(step):
        for block in range(2):
            for f in range(2):
                index = (step * 2 + block) * 2 + f
                slot = kv_recv.at[step, block, f]
                if step or f:
                    remote(slot, slot, kv_s.at[index], kv_r.at[index], (ctx, head)).wait_recv()
        for block in range(2):
            for f in range(2):
                index = (step * 2 + block) * 2 + f
                place = slice(index * BLK, (index + 1) * BLK)
                k = kv_recv[step, block, f, 0]
                hidden = jnp.broadcast_to(bias[step, block, f][0:1].astype(BF16), k.shape)
                k_aug[0, place] = jnp.where(low, k, hidden)
                k_aug[1, place] = jnp.where(low, hidden, k)
                v = kv_recv[step, block, f, 1].astype(F32).T.astype(BF16)
                for h in range(2):
                    v_aug[h, 0:HS, place] = v[h * HS:(h + 1) * HS]
                    v_aug[h, HS:PACK, place] = jnp.ones((PACK - HS, BLK), BF16)

    def product(keys, queries):
        return lax.dot_general(keys, queries, (((1,), (1,)), ((), ())), preferred_element_type=F32)

    def first_group(step, first):
        build_keys(step)
        keys = slice(step * 4 * BLK, (step + 1) * 4 * BLK)
        for h in range(2):
            s = product(k_aug[h, keys], q_aug[h, 0:group])
            top = jnp.max(s, axis=0, keepdims=True)
            if not first:
                old = top_ref[h, 0:1]
                top = jnp.maximum(top, old)
            part = jnp.dot(v_aug[h, :, keys], jnp.exp2(s - top).astype(BF16), preferred_element_type=F32)
            if not first:
                part = part + acc[h] * jnp.exp2(old - top)
            acc[h] = part
            top_ref[h, 0:1] = top

    build_queries(0)
    for step in near_first(ny):
        first_group(step, step == 0)

    units = [(dx, h) for dx in x_far for h in range(2)]
    buffers = (scores_0, scores_1)

    def score(u):
        dx, h = units[u]
        if h == 0:
            build_queries(dx)
        s = product(k_aug[h], q_aug[h, dx * group:(dx + 1) * group])
        buffers[u % 2][...] = s
        return jnp.max(s, axis=0, keepdims=True)

    top = score(0)
    for u, (dx, h) in enumerate(units):
        later = score(u + 1) if u + 1 < len(units) else None
        weights = jnp.exp2(buffers[u % 2][...] - top).astype(BF16)
        part = jnp.dot(v_aug[h], weights, preferred_element_type=F32)
        a_send[dx, h, 0:HS] = part[0:HS].astype(BF16)
        a_send[dx, h, HS:PACK] = pack_stats(top, part[HS:HS + 1])
        index = 2 * dx + h
        push(
            a_send.at[dx, h], a_recv.at[dx, h], a_s.at[index], a_r.at[index],
            (down(x, dx, nx) * nz + z, head),
        )
        top = later

    packed = []
    for h in range(2):
        tops, totals = [top_ref[h, 0:1]], [acc[h, HS:HS + 1]]
        for dx in x_far:
            index = 2 * dx + h
            slot = a_recv.at[dx, h]
            remote(slot, slot, a_s.at[index], a_r.at[index], (ctx, head)).wait_recv()
            one_top, one_total = unpack_stats(a_recv[dx, h, HS:PACK])
            tops.append(one_top)
            totals.append(one_total)
        top = functools.reduce(jnp.maximum, tops)
        factors = [jnp.exp2(one - top) for one in tops]
        total = sum(one * factor for one, factor in zip(totals, factors))
        value = acc[h, 0:HS] * factors[0]
        for dx, factor in zip(x_far, factors[1:]):
            value = value + a_recv[dx, h, 0:HS].astype(F32) * factor
        packed.append((value, pack_stats(top, total).astype(F32)))
    for t in range(group // LANES):
        cols = slice(t * LANES, (t + 1) * LANES)
        for part, place in ((0, slice(0, HS)), (1, slice(HS, PACK))):
            a, b = packed[0][part][:, cols], packed[1][part][:, cols]
            p_send[2 * t, place] = jnp.where(low, a, pltpu.roll(b, HS, 1)).astype(BF16)
            p_send[2 * t + 1, place] = jnp.where(low, pltpu.roll(a, HS, 1), b).astype(BF16)

    def p_copy(dz):
        return remote(p_send.at[dz], p_recv.at[dz], p_s.at[dz], p_r.at[dz], owner(dz))

    for dz in z_far + [0]:
        other_device(dz, lambda: p_copy(dz).start())

    @pl.when(at_home)
    def _():
        p_recv[0] = p_send[0]

    for dz in z_far + [0]:
        slot = p_recv.at[dz]
        other_device(dz, lambda: remote(slot, slot, p_s.at[dz], p_r.at[dz], (ctx, head)).wait_recv())
    messages = [p_recv[dz] for dz in range(nz)]
    stats = [unpack_stats(message[HS:PACK]) for message in messages]
    top = functools.reduce(jnp.maximum, [one for one, _ in stats])
    factors = [jnp.exp2(one - top) for one, _ in stats]
    total = sum(one * factor for (_, one), factor in zip(stats, factors))
    value = sum(message[0:HS].astype(F32) * factor for message, factor in zip(messages, factors))
    load_ow.wait()
    attended = (value / total).T.astype(BF16)
    mixed = jnp.dot(attended[0:own], ow[0:HS], preferred_element_type=F32) + jnp.dot(
        attended[own:2 * own], ow[HS:2 * HS], preferred_element_type=F32
    )

    each = own // heads
    half = width // 2
    for h in range(heads):
        rows = mixed[h * each:(h + 1) * each]
        fin_send[h] = jnp.concatenate([rows[:, :half], rows[:, half:]], axis=0).astype(BF16)
    h_steps = range(1, heads)
    for step in h_steps:
        hd = up(head, step, heads)
        push(fin_send.at[hd], fin_recv.at[step], fin_s.at[step], fin_r.at[step], (ctx, hd))
    result = fin_send[head].astype(F32)
    for step in h_steps:
        slot = fin_recv.at[step]
        remote(slot, slot, fin_s.at[step], fin_r.at[step], (ctx, head)).wait_recv()
        result = result + fin_recv[step].astype(F32)
    out_ref[...] = jnp.concatenate([result[0:each], result[each:2 * each]], axis=1).astype(out_ref.dtype)
    for copy in sent:
        copy.wait_send()
    for dz in z_far + [0]:
        other_device(dz, lambda: q_copy(dz).wait_send())
        other_device(dz, lambda: p_copy(dz).wait_send())


def per_device(nx, nz, ny, latents, frames, block_lists, query_weight, key_weight, value_weight, output_weight):
    own, depth = latents.shape
    count = frames.shape[0]
    width = output_weight.shape[1]
    heads, group = 2 * ny, nz * own
    rows = nx * group
    keys = ny * 4 * BLK
    each = own // heads
    any_space, vmem = pl.BlockSpec(memory_space=pl.ANY), pl.BlockSpec(memory_space=pltpu.VMEM)
    dma = pltpu.SemaphoreType.DMA
    return pl.pallas_call(
        functools.partial(kernel, nx, nz, ny),
        out_shape=jax.ShapeDtypeStruct((each, width), BF16),
        in_specs=[any_space] * 7,
        out_specs=vmem,
        scratch_shapes=[
            pltpu.VMEM((own, depth), BF16),
            pltpu.VMEM((count, depth), BF16),
            pltpu.VMEM(block_lists.shape, jnp.int32),
            pltpu.VMEM((depth, LANES), BF16),
            pltpu.VMEM((ny, depth, 2 * LANES), BF16),
            pltpu.VMEM((ny, depth, 2 * LANES), BF16),
            pltpu.VMEM((LANES, width), BF16),
            pltpu.VMEM((ny, 2, 2, 8, LANES), F32),
            pltpu.VMEM((own, LANES), BF16),
            pltpu.VMEM((nx, nz, own, LANES), BF16),
            pltpu.VMEM((2, rows, LANES), BF16),
            pltpu.VMEM((ny, 2, 2, 2, BLK, LANES), BF16),
            pltpu.VMEM((ny, 2, 2, 2, BLK, LANES), BF16),
            pltpu.VMEM((2, keys, LANES), BF16),
            pltpu.VMEM((2, PACK, keys), BF16),
            pltpu.VMEM((keys, group), F32),
            pltpu.VMEM((keys, group), F32),
            pltpu.VMEM((2, 8, group), F32),
            pltpu.VMEM((2, PACK, group), F32),
            pltpu.VMEM((nx, 2, PACK, group), BF16),
            pltpu.VMEM((nx, 2, PACK, group), BF16),
            pltpu.VMEM((nz, PACK, LANES), BF16),
            pltpu.VMEM((nz, PACK, LANES), BF16),
            pltpu.VMEM((heads, 2 * each, width // 2), BF16),
            pltpu.VMEM((heads, 2 * each, width // 2), BF16),
            dma((5 + 2 * ny,)),
            dma((nz,)), dma((nz,)),
            dma((nx * nz,)), dma((nx * nz,)),
            dma((4 * ny,)), dma((4 * ny,)),
            dma((2 * nx,)), dma((2 * nx,)),
            dma((nz,)), dma((nz,)),
            dma((heads,)), dma((heads,)),
        ],
        compiler_params=pltpu.CompilerParams(
            collective_id=0, has_side_effects=True, vmem_limit_bytes=56 * 2**20
        ),
        name="cross_attention",
    )(latents, frames, block_lists, query_weight, key_weight, value_weight, output_weight)


def solution(mesh, nx=4, nz=8, ny=4):
    return jax.shard_map(
        functools.partial(per_device, nx, nz, ny),
        mesh=mesh,
        in_specs=(
            P("ctx", None),
            P(("ctx", "head"), None),
            P(),
            P(None, "head"),
            P(),
            P(),
            P("head", None),
        ),
        out_specs=P(("ctx", "head"), None),
        check_vma=False,
    )
```

time: 62 us -> 53.2 us (0.86)
  Pallas kernels: 60.4 us -> 51.7 us
    pallas_call x1, Pallas kernels: 60.4 us -> 51.7 us  [per_device(): pl.pallas_call(functools.partial(kernel, nx, nz, ny), out_shape=jax.Shape...]
where the time goes in v3:
time: 53.2 us; the launch traced here: 53 us
  Pallas kernels  51.7 us (97%)
  local copies, waits for them, and re-layouts  1.32 us (2%)
    pallas_call x1, Pallas kernels, per_device(): pl.pallas_call(functools.partial(kernel, nx, nz, ny), out_shape=jax.Shape...  51.7 us
    unnamed x1, local copies, waits for them, and re-layouts  1.32 us

profile of v3, /device:TPU:1, one launch (start us, length us, event | category | flops | bytes accessed | tf_op | source)
XLA Modules:
  0.0 53.0 jit_solution(16274767612815661466)
XLA Ops:
  0.0 51.7 %cross_attention.1 = bf16[8,1024]{1,0:T(8,128)(2,1)} custom-call(bf16[64,1024]{1,0:T(8,128)(2,1)} %lat_hbm.1, bf16[256,1024]{1,0:T(8,128)(2,1)} %fr_hbm.1, s32[16,256]{1,0:T(8,128)} %lists_hbm.1, bf16[1024,128]{1,0:T(8,128)(2,1)} %qw_hbm.1, bf16[1024,1024]{1,0:T(8,128)(2,1)} %kw_hbm.1, bf16[1024,1024]{1,0:T(8,128)(2,1)} %vw_hbm.1, bf16[128,1024]{1,0:T(8,128)(2,1)} %ow_hbm.1), custom_call_target="tpu_custom_call" | custom-call | tf_op jit(solution)/shard_map/cross_attention/pallas_call | solution.py:378
  51.7 1.3 %copy.9 = bf16[8,1024]{1,0:T(8,128)(2,1)} copy(bf16[8,1024]{1,0:T(8,128)(2,1)} %cross_attention.1) | data formatting | bytes 32768

commit v4 on v3

--- a/solution.py
+++ b/solution.py
@@ -11,6 +11,7 @@
 BLK = 128
 LANES = 2 * HS
 PACK = HS + 16
+HALF = HS // 2
 SCALE = HS ** (-0.5) * 1.4426950408889634
 NEG = -1e30
 MESH = pl.DeviceIdType.MESH
@@ -61,6 +62,8 @@
     heads = 2 * ny
     own = lat.shape[0]
     group = nz * own
+    parts = a_recv.shape[2]
+    chunk = group // parts
     width = out_ref.shape[1]
     quarter = lax.rem(y + z, ny)
     at_home = lax.rem(z, ny) == 0
@@ -269,100 +272,133 @@
     for step in near_first(ny):
         first_group(step, step == 0)
 
-    units = [(dx, h) for dx in x_far for h in range(2)]
+    units = [(h, dx, part) for h in range(2) for dx in x_far for part in range(parts)]
     buffers = (scores_0, scores_1)
-
-    def score(u):
-        dx, h = units[u]
-        if h == 0:
-            build_queries(dx)
-        s = product(k_aug[h], q_aug[h, dx * group:(dx + 1) * group])
-        buffers[u % 2][...] = s
+    keys = v_aug.shape[2]
+    halves = [slice(0, keys // 2), slice(keys // 2, keys)]
+
+    def scored(u, place):
+        h, dx, part = units[u]
+        first = dx * group + part * chunk
+        s = product(k_aug[h, place], q_aug[h, first:first + chunk])
+        buffers[u % 2][place] = s
         return jnp.max(s, axis=0, keepdims=True)
 
-    top = score(0)
-    for u, (dx, h) in enumerate(units):
-        later = score(u + 1) if u + 1 < len(units) else None
-        weights = jnp.exp2(buffers[u % 2][...] - top).astype(BF16)
-        part = jnp.dot(v_aug[h], weights, preferred_element_type=F32)
-        a_send[dx, h, 0:HS] = part[0:HS].astype(BF16)
-        a_send[dx, h, HS:PACK] = pack_stats(top, part[HS:HS + 1])
-        index = 2 * dx + h
+    def weighed(u, place, top):
+        weights = jnp.exp2(buffers[u % 2][place] - top).astype(BF16)
+        return jnp.dot(v_aug[units[u][0], :, place], weights, preferred_element_type=F32)
+
+    def send_unit(u, top, value):
+        h, dx, part = units[u]
+        a_send[dx, h, part, 0:HS] = value[0:HS].astype(BF16)
+        a_send[dx, h, part, HS:PACK] = pack_stats(top, value[HS:HS + 1])
+        index = (dx * 2 + h) * parts + part
         push(
-            a_send.at[dx, h], a_recv.at[dx, h], a_s.at[index], a_r.at[index],
+            a_send.at[dx, h, part], a_recv.at[dx, h, part], a_s.at[index], a_r.at[index],
             (down(x, dx, nx) * nz + z, head),
         )
-        top = later
-
-    packed = []
-    for h in range(2):
-        tops, totals = [top_ref[h, 0:1]], [acc[h, HS:HS + 1]]
-        for dx in x_far:
-            index = 2 * dx + h
-            slot = a_recv.at[dx, h]
-            remote(slot, slot, a_s.at[index], a_r.at[index], (ctx, head)).wait_recv()
-            one_top, one_total = unpack_stats(a_recv[dx, h, HS:PACK])
-            tops.append(one_top)
-            totals.append(one_total)
-        top = functools.reduce(jnp.maximum, tops)
-        factors = [jnp.exp2(one - top) for one in tops]
-        total = sum(one * factor for one, factor in zip(totals, factors))
-        value = acc[h, 0:HS] * factors[0]
-        for dx, factor in zip(x_far, factors[1:]):
-            value = value + a_recv[dx, h, 0:HS].astype(F32) * factor
-        packed.append((value, pack_stats(top, total).astype(F32)))
-    for t in range(group // LANES):
-        cols = slice(t * LANES, (t + 1) * LANES)
-        for part, place in ((0, slice(0, HS)), (1, slice(HS, PACK))):
-            a, b = packed[0][part][:, cols], packed[1][part][:, cols]
-            p_send[2 * t, place] = jnp.where(low, a, pltpu.roll(b, HS, 1)).astype(BF16)
-            p_send[2 * t + 1, place] = jnp.where(low, pltpu.roll(a, HS, 1), b).astype(BF16)
-
-    def p_copy(dz):
-        return remote(p_send.at[dz], p_recv.at[dz], p_s.at[dz], p_r.at[dz], owner(dz))
-
-    for dz in z_far + [0]:
-        other_device(dz, lambda: p_copy(dz).start())
-
-    @pl.when(at_home)
-    def _():
-        p_recv[0] = p_send[0]
-
-    for dz in z_far + [0]:
-        slot = p_recv.at[dz]
-        other_device(dz, lambda: remote(slot, slot, p_s.at[dz], p_r.at[dz], (ctx, head)).wait_recv())
-    messages = [p_recv[dz] for dz in range(nz)]
-    stats = [unpack_stats(message[HS:PACK]) for message in messages]
-    top = functools.reduce(jnp.maximum, [one for one, _ in stats])
-    factors = [jnp.exp2(one - top) for one, _ in stats]
-    total = sum(one * factor for (_, one), factor in zip(stats, factors))
-    value = sum(message[0:HS].astype(F32) * factor for message, factor in zip(messages, factors))
+
+    top = None
+    for u in range(-1, len(units)):
+        tops, values = [], []
+        if u + 1 < len(units):
+            h, dx, part = units[u + 1]
+            if h == 0 and part == 0:
+                build_queries(dx)
+        for place in halves:
+            if u + 1 < len(units):
+                tops.append(scored(u + 1, place))
+            if u >= 0:
+                values.append(weighed(u, place, top))
+        if values:
+            send_unit(u, top, values[0] + values[1])
+        if tops:
+            top = jnp.maximum(tops[0], tops[1])
+
+    def merge_x(h):
+        for part in range(parts):
+            span = slice(part * chunk, (part + 1) * chunk)
+            tops, totals = [top_ref[h, 0:1, span]], [acc[h, HS:HS + 1, span]]
+            for dx in x_far:
+                index = (dx * 2 + h) * parts + part
+                slot = a_recv.at[dx, h, part]
+                remote(slot, slot, a_s.at[index], a_r.at[index], (ctx, head)).wait_recv()
+                one_top, one_total = unpack_stats(a_recv[dx, h, part, HS:PACK])
+                tops.append(one_top)
+                totals.append(one_total)
+            top = functools.reduce(jnp.maximum, tops)
+            factors = [jnp.exp2(one - top) for one in tops]
+            total = sum(one * factor for one, factor in zip(totals, factors))
+            value = acc[h, 0:HS, span] * factors[0]
+            for dx, factor in zip(x_far, factors[1:]):
+                value = value + a_recv[dx, h, part, 0:HS].astype(F32) * factor
+            stats = pack_stats(top, total).astype(F32)
+            for t in range(chunk // LANES):
+                cols = slice(t * LANES, (t + 1) * LANES)
+                dz = 2 * (part * (chunk // LANES) + t)
+                for a, b, place in (
+                    (value[0:HALF, cols], value[HALF:HS, cols], slice(0, HALF)),
+                    (stats[:, cols], stats[:, cols], slice(HALF, HALF + 16)),
+                ):
+                    p_send[h, dz, place] = jnp.where(low, a, pltpu.roll(b, HS, 1)).astype(BF16)
+                    p_send[h, dz + 1, place] = jnp.where(low, pltpu.roll(a, HS, 1), b).astype(BF16)
+        for dz in z_far + [0]:
+            other_device(dz, lambda: p_copy(h, dz).start())
+
+        @pl.when(at_home)
+        def _():
+            p_recv[h, 0] = p_send[h, 0]
+
+    def p_copy(h, dz):
+        index = h * nz + dz
+        return remote(p_send.at[h, dz], p_recv.at[h, dz], p_s.at[index], p_r.at[index], owner(dz))
+
+    def merge_z(h):
+        for dz in z_far + [0]:
+            index = h * nz + dz
+            slot = p_recv.at[h, dz]
+            other_device(
+                dz, lambda: remote(slot, slot, p_s.at[index], p_r.at[index], (ctx, head)).wait_recv()
+            )
+        stats = [unpack_stats(p_recv[h, dz, HALF:HALF + 16]) for dz in range(nz)]
+        top = functools.reduce(jnp.maximum, [one for one, _ in stats])
+        factors = [jnp.exp2(one - top) for one, _ in stats]
+        total = sum(one * factor for (_, one), factor in zip(stats, factors))
+        value = sum(p_recv[h, dz, 0:HALF].astype(F32) * factors[dz] for dz in range(nz))
+        attended = (value / total).T.astype(BF16)
+        return jnp.dot(attended[0:own], ow[h * HS:h * HS + HALF], preferred_element_type=F32) + jnp.dot(
+            attended[own:2 * own], ow[h * HS + HALF:(h + 1) * HS], preferred_element_type=F32
+        )
+
+    merge_x(0)
+    merge_x(1)
     load_ow.wait()
-    attended = (value / total).T.astype(BF16)
-    mixed = jnp.dot(attended[0:own], ow[0:HS], preferred_element_type=F32) + jnp.dot(
-        attended[own:2 * own], ow[HS:2 * HS], preferred_element_type=F32
-    )
+    mixed = merge_z(0)
+    mixed = mixed + merge_z(1)
 
     each = own // heads
     half = width // 2
     for h in range(heads):
         rows = mixed[h * each:(h + 1) * each]
         fin_send[h] = jnp.concatenate([rows[:, :half], rows[:, half:]], axis=0).astype(BF16)
-    h_steps = range(1, heads)
-    for step in h_steps:
-        hd = up(head, step, heads)
-        push(fin_send.at[hd], fin_recv.at[step], fin_s.at[step], fin_r.at[step], (ctx, hd))
+    ways = [(step, f) for step in far_first(ny) + [0] for f in range(2) if step or f]
+    for step, f in ways:
+        hd = 2 * up(y, step, ny) + core_of(f)
+        index = 2 * step + f
+        push(fin_send.at[hd], fin_recv.at[index], fin_s.at[index], fin_r.at[index], (ctx, hd))
     result = fin_send[head].astype(F32)
-    for step in h_steps:
-        slot = fin_recv.at[step]
-        remote(slot, slot, fin_s.at[step], fin_r.at[step], (ctx, head)).wait_recv()
-        result = result + fin_recv[step].astype(F32)
+    for step, f in ways[::-1]:
+        index = 2 * step + f
+        slot = fin_recv.at[index]
+        remote(slot, slot, fin_s.at[index], fin_r.at[index], (ctx, head)).wait_recv()
+        result = result + fin_recv[index].astype(F32)
     out_ref[...] = jnp.concatenate([result[0:each], result[each:2 * each]], axis=1).astype(out_ref.dtype)
     for copy in sent:
         copy.wait_send()
     for dz in z_far + [0]:
         other_device(dz, lambda: q_copy(dz).wait_send())
-        other_device(dz, lambda: p_copy(dz).wait_send())
+        for h in range(2):
+            other_device(dz, lambda: p_copy(h, dz).wait_send())
 
 
 def per_device(nx, nz, ny, latents, frames, block_lists, query_weight, key_weight, value_weight, output_weight):
@@ -372,6 +408,7 @@
     heads, group = 2 * ny, nz * own
     rows = nx * group
     keys = ny * 4 * BLK
+    parts = 2 if group >= 4 * HS else 1
     each = own // heads
     any_space, vmem = pl.BlockSpec(memory_space=pl.ANY), pl.BlockSpec(memory_space=pltpu.VMEM)
     dma = pltpu.SemaphoreType.DMA
@@ -396,22 +433,22 @@
             pltpu.VMEM((ny, 2, 2, 2, BLK, LANES), BF16),
             pltpu.VMEM((2, keys, LANES), BF16),
             pltpu.VMEM((2, PACK, keys), BF16),
-            pltpu.VMEM((keys, group), F32),
-            pltpu.VMEM((keys, group), F32),
+            pltpu.VMEM((keys, group // parts), F32),
+            pltpu.VMEM((keys, group // parts), F32),
             pltpu.VMEM((2, 8, group), F32),
             pltpu.VMEM((2, PACK, group), F32),
-            pltpu.VMEM((nx, 2, PACK, group), BF16),
-            pltpu.VMEM((nx, 2, PACK, group), BF16),
-            pltpu.VMEM((nz, PACK, LANES), BF16),
-            pltpu.VMEM((nz, PACK, LANES), BF16),
+            pltpu.VMEM((nx, 2, parts, PACK, group // parts), BF16),
+            pltpu.VMEM((nx, 2, parts, PACK, group // parts), BF16),
+            pltpu.VMEM((2, nz, HALF + 16, LANES), BF16),
+            pltpu.VMEM((2, nz, HALF + 16, LANES), BF16),
             pltpu.VMEM((heads, 2 * each, width // 2), BF16),
             pltpu.VMEM((heads, 2 * each, width // 2), BF16),
             dma((5 + 2 * ny,)),
             dma((nz,)), dma((nz,)),
             dma((nx * nz,)), dma((nx * nz,)),
             dma((4 * ny,)), dma((4 * ny,)),
-            dma((2 * nx,)), dma((2 * nx,)),
-            dma((nz,)), dma((nz,)),
+            dma((2 * nx * parts,)), dma((2 * nx * parts,)),
+            dma((2 * nz,)), dma((2 * nz,)),
             dma((heads,)), dma((heads,)),
         ],
         compiler_params=pltpu.CompilerParams(

time: 53.2 us -> 52 us (0.977)
  Pallas kernels: 51.7 us -> 50.5 us
    pallas_call x1, Pallas kernels: 51.7 us -> 50.5 us  [per_device(): pl.pallas_call(functools.partial(kernel, nx, nz, ny), out_shape=jax.Shape...]
where the time goes in v4:
time: 52 us; the launch traced here: 51.8 us
  Pallas kernels  50.5 us (97%)
  local copies, waits for them, and re-layouts  1.32 us (3%)
    pallas_call x1, Pallas kernels, per_device(): pl.pallas_call(functools.partial(kernel, nx, nz, ny), out_shape=jax.Shape...  50.5 us
    unnamed x1, local copies, waits for them, and re-layouts  1.32 us

profile of v4, /device:TPU:1, one launch (start us, length us, event | category | flops | bytes accessed | tf_op | source)
XLA Modules:
  0.0 51.8 jit_solution(11560570988054747850)
XLA Ops:
  0.0 50.5 %cross_attention.1 = bf16[8,1024]{1,0:T(8,128)(2,1)} custom-call(bf16[64,1024]{1,0:T(8,128)(2,1)} %lat_hbm.1, bf16[256,1024]{1,0:T(8,128)(2,1)} %fr_hbm.1, s32[16,256]{1,0:T(8,128)} %lists_hbm.1, bf16[1024,128]{1,0:T(8,128)(2,1)} %qw_hbm.1, bf16[1024,1024]{1,0:T(8,128)(2,1)} %kw_hbm.1, bf16[1024,1024]{1,0:T(8,128)(2,1)} %vw_hbm.1, bf16[128,1024]{1,0:T(8,128)(2,1)} %ow_hbm.1), custom_call_target="tpu_custom_call" | custom-call | tf_op jit(solution)/shard_map/cross_attention/pallas_call | solution.py:415
  50.5 1.3 %copy.9 = bf16[8,1024]{1,0:T(8,128)(2,1)} copy(bf16[8,1024]{1,0:T(8,128)(2,1)} %cross_attention.1) | data formatting | bytes 32768

commit v5 on v4

--- a/solution.py
+++ b/solution.py
@@ -74,6 +74,55 @@
     def down(value, step, count):
         return lax.rem(value + count - step, count)
 
+    def user(dz):
+        zt = up(z, dz, nz)
+        return (x * nz + zt, 2 * down(y, lax.rem(zt, ny), ny) + c)
+
+    def owner(dz):
+        return (x * nz + down(z, dz, nz), 2 * quarter + c)
+
+    def other_device(dz, action):
+        if dz:
+            action()
+        else:
+            pl.when(jnp.logical_not(at_home))(action)
+
+    def z_steps(step, core):
+        if step in (0, 1):
+            return step
+        if step == ny - 1:
+            return nz - 1
+        return step + core * (nz - 2 * step)
+
+    def core_of(f):
+        return c if f == 0 else 1 - c
+
+    def frames_to(step, block, f):
+        if block == 0:
+            return (ctx, 2 * up(y, step, ny) + core_of(f))
+        return (x * nz + up(z, z_steps(step, c), nz), 2 * y + core_of(f))
+
+    def frames_from(step, block, f):
+        if block == 0:
+            return (ctx, 2 * down(y, step, ny) + core_of(f))
+        return (x * nz + down(z, z_steps(step, core_of(f)), nz), 2 * y + core_of(f))
+
+    barrier = pltpu.get_barrier_semaphore()
+
+    def greet(device):
+        pl.semaphore_signal(barrier, inc=1, device_id=device, device_id_type=MESH)
+
+    z_far, x_far = far_first(nz), far_first(nx)
+    for dz in z_far + [0]:
+        other_device(dz, lambda: greet(owner(dz)))
+    for dx in x_far:
+        greet((down(x, dx, nx) * nz + z, head))
+    for step in far_first(ny):
+        for block in range(2):
+            for f in range(2):
+                greet(frames_from(step, block, f))
+    greet((ctx, 2 * y + 1 - c))
+
     loads = []
 
     def load(src, dst):
@@ -93,58 +142,23 @@
         load_kv.append((load(kw_hbm.at[:, cols], kw.at[step]), load(vw_hbm.at[:, cols], vw.at[step])))
     load_ow = load(ow_hbm, ow)
 
-    def user(dz):
-        zt = up(z, dz, nz)
-        return (x * nz + zt, 2 * down(y, lax.rem(zt, ny), ny) + c)
-
-    def owner(dz):
-        return (x * nz + down(z, dz, nz), 2 * quarter + c)
-
-    def other_device(dz, action):
-        if dz:
-            action()
-        else:
-            pl.when(jnp.logical_not(at_home))(action)
-
-    def z_steps(step, core):
-        if step in (0, 1):
-            return step
-        if step == ny - 1:
-            return nz - 1
-        return step + core * (nz - 2 * step)
-
-    def core_of(f):
-        return c if f == 0 else 1 - c
-
-    def frames_to(step, block, f):
-        if block == 0:
-            return (ctx, 2 * up(y, step, ny) + core_of(f))
-        return (x * nz + up(z, z_steps(step, c), nz), 2 * y + core_of(f))
-
-    def frames_from(step, block, f):
-        if block == 0:
-            return (ctx, 2 * down(y, step, ny) + core_of(f))
-        return (x * nz + down(z, z_steps(step, core_of(f)), nz), 2 * y + core_of(f))
-
-    barrier = pltpu.get_barrier_semaphore()
-
-    def greet(device):
-        pl.semaphore_signal(barrier, inc=1, device_id=device, device_id_type=MESH)
-
-    z_far, x_far = far_first(nz), far_first(nx)
-    for dz in z_far + [0]:
-        other_device(dz, lambda: greet(owner(dz)))
-    for dx in x_far:
-        greet((down(x, dx, nx) * nz + z, head))
-    for step in far_first(ny):
-        for block in range(2):
-            for f in range(2):
-                greet(frames_from(step, block, f))
-    greet((ctx, 2 * y + 1 - c))
-
     load_lat.wait()
     load_qw.wait()
     q_own[...] = (jnp.dot(lat[...], qw[...], preferred_element_type=F32) * SCALE).astype(BF16)
+    def project_frames(i):
+        step = y_order[i]
+        for copy in load_kv[i]:
+            copy.wait()
+        for part, weight in ((0, kw), (1, vw)):
+            rows = jnp.dot(fr[...], weight[step], preferred_element_type=F32).astype(BF16)
+            for block in range(2):
+                for cd in range(2):
+                    kv_send[step, block, cd, part] = rows[
+                        block * BLK:(block + 1) * BLK, cd * LANES:(cd + 1) * LANES
+                    ]
+
+    load_fr.wait()
+    project_frames(0)
     greeted = nz - 1 + nx - 1 + 4 * (ny - 1) + 1
     pl.semaphore_wait(barrier, greeted + jnp.minimum(lax.rem(z, ny), 1))
 
@@ -183,17 +197,9 @@
                 seen = jnp.max(jnp.where(lists == block_id, 1.0, 0.0), axis=0, keepdims=True)
                 bias[step, block, f] = jnp.broadcast_to(jnp.where(seen > 0.0, 0.0, NEG), (8, LANES))
 
-    load_fr.wait()
     for i, step in enumerate(y_order):
-        for copy in load_kv[i]:
-            copy.wait()
-        for part, weight in ((0, kw), (1, vw)):
-            rows = jnp.dot(fr[...], weight[step], preferred_element_type=F32).astype(BF16)
-            for block in range(2):
-                for cd in range(2):
-                    kv_send[step, block, cd, part] = rows[
-                        block * BLK:(block + 1) * BLK, cd * LANES:(cd + 1) * LANES
-                    ]
+        if i:
+            project_frames(i)
         for f in range(2):
             for block in range(2):
                 index = (step * 2 + block) * 2 + f
@@ -253,26 +259,12 @@
     def product(keys, queries):
         return lax.dot_general(keys, queries, (((1,), (1,)), ((), ())), preferred_element_type=F32)
 
-    def first_group(step, first):
-        build_keys(step)
-        keys = slice(step * 4 * BLK, (step + 1) * 4 * BLK)
-        for h in range(2):
-            s = product(k_aug[h, keys], q_aug[h, 0:group])
-            top = jnp.max(s, axis=0, keepdims=True)
-            if not first:
-                old = top_ref[h, 0:1]
-                top = jnp.maximum(top, old)
-            part = jnp.dot(v_aug[h, :, keys], jnp.exp2(s - top).astype(BF16), preferred_element_type=F32)
-            if not first:
-                part = part + acc[h] * jnp.exp2(old - top)
-            acc[h] = part
-            top_ref[h, 0:1] = top
-
     build_queries(0)
     for step in near_first(ny):
-        first_group(step, step == 0)
+        build_keys(step)
 
     units = [(h, dx, part) for h in range(2) for dx in x_far for part in range(parts)]
+    units += [(h, 0, part) for h in range(2) for part in range(parts)]
     buffers = (scores_0, scores_1)
     keys = v_aug.shape[2]
     halves = [slice(0, keys // 2), slice(keys // 2, keys)]
@@ -288,8 +280,13 @@
         weights = jnp.exp2(buffers[u % 2][place] - top).astype(BF16)
         return jnp.dot(v_aug[units[u][0], :, place], weights, preferred_element_type=F32)
 
-    def send_unit(u, top, value):
+    def finish_unit(u, top, value):
         h, dx, part = units[u]
+        if dx == 0:
+            span = slice(part * chunk, (part + 1) * chunk)
+            acc[h, :, span] = value
+            top_ref[h, 0:1, span] = top
+            return
         a_send[dx, h, part, 0:HS] = value[0:HS].astype(BF16)
         a_send[dx, h, part, HS:PACK] = pack_stats(top, value[HS:HS + 1])
         index = (dx * 2 + h) * parts + part
@@ -297,23 +294,6 @@
             a_send.at[dx, h, part], a_recv.at[dx, h, part], a_s.at[index], a_r.at[index],
             (down(x, dx, nx) * nz + z, head),
         )
-
-    top = None
-    for u in range(-1, len(units)):
-        tops, values = [], []
-        if u + 1 < len(units):
-            h, dx, part = units[u + 1]
-            if h == 0 and part == 0:
-                build_queries(dx)
-        for place in halves:
-            if u + 1 < len(units):
-                tops.append(scored(u + 1, place))
-            if u >= 0:
-                values.append(weighed(u, place, top))
-        if values:
-            send_unit(u, top, values[0] + values[1])
-        if tops:
-            top = jnp.maximum(tops[0], tops[1])
 
     def merge_x(h):
         for part in range(parts):
@@ -370,7 +350,25 @@
             attended[own:2 * own], ow[h * HS + HALF:(h + 1) * HS], preferred_element_type=F32
         )
 
-    merge_x(0)
+    top = None
+    for u in range(-1, len(units)):
+        tops, values = [], []
+        if u + 1 < len(units):
+            h, dx, part = units[u + 1]
+            if h == 0 and part == 0 and dx:
+                build_queries(dx)
+        for place in halves:
+            if u + 1 < len(units):
+                tops.append(scored(u + 1, place))
+            if u >= 0:
+                values.append(weighed(u, place, top))
+        if values:
+            finish_unit(u, top, values[0] + values[1])
+            if units[u] == (0, 0, parts - 1):
+                merge_x(0)
+        if tops:
+            top = jnp.maximum(tops[0], tops[1])
+
     merge_x(1)
     load_ow.wait()
     mixed = merge_z(0)

time: 52 us -> 48.5 us (0.933)
  Pallas kernels: 50.5 us -> 47 us
    pallas_call x1, Pallas kernels: 50.5 us -> 47 us  [per_device(): pl.pallas_call(functools.partial(kernel, nx, nz, ny), out_shape=jax.Shape...]
where the time goes in v5:
time: 48.5 us; the launch traced here: 48.4 us
  Pallas kernels  47 us (97%)
  local copies, waits for them, and re-layouts  1.32 us (3%)
    pallas_call x1, Pallas kernels, per_device(): pl.pallas_call(functools.partial(kernel, nx, nz, ny), out_shape=jax.Shape...  47 us
    unnamed x1, local copies, waits for them, and re-layouts  1.32 us

profile of v5, /device:TPU:1, one launch (start us, length us, event | category | flops | bytes accessed | tf_op | source)
XLA Modules:
  0.0 48.4 jit_solution(7629213624218130323)
XLA Ops:
  0.0 47.0 %cross_attention.1 = bf16[8,1024]{1,0:T(8,128)(2,1)} custom-call(bf16[64,1024]{1,0:T(8,128)(2,1)} %lat_hbm.1, bf16[256,1024]{1,0:T(8,128)(2,1)} %fr_hbm.1, s32[16,256]{1,0:T(8,128)} %lists_hbm.1, bf16[1024,128]{1,0:T(8,128)(2,1)} %qw_hbm.1, bf16[1024,1024]{1,0:T(8,128)(2,1)} %kw_hbm.1, bf16[1024,1024]{1,0:T(8,128)(2,1)} %vw_hbm.1, bf16[128,1024]{1,0:T(8,128)(2,1)} %ow_hbm.1), custom_call_target="tpu_custom_call" | custom-call | tf_op jit(solution)/shard_map/cross_attention/pallas_call | solution.py:413
  47.0 1.3 %copy.9 = bf16[8,1024]{1,0:T(8,128)(2,1)} copy(bf16[8,1024]{1,0:T(8,128)(2,1)} %cross_attention.1) | data formatting | bytes 32768

commit v6 on v5

--- a/solution.py
+++ b/solution.py
@@ -184,19 +184,6 @@
     def _():
         q_recv[0, 0] = q_own[...]
 
-    load_lists.wait()
-    lists = lists_ref[...].astype(F32)
-    blocks, listed = lists.shape
-    unused = jnp.full((HS - blocks, listed), -1.0, F32)
-    lists = jnp.concatenate([lists, unused, lists, unused], axis=0).T
-    for step in range(ny):
-        for block in range(2):
-            for f in range(2):
-                from_ctx, from_head = frames_from(step, block, f)
-                block_id = ((from_ctx * heads + from_head) * 2 + block).astype(F32)
-                seen = jnp.max(jnp.where(lists == block_id, 1.0, 0.0), axis=0, keepdims=True)
-                bias[step, block, f] = jnp.broadcast_to(jnp.where(seen > 0.0, 0.0, NEG), (8, LANES))
-
     for i, step in enumerate(y_order):
         if i:
             project_frames(i)
@@ -217,6 +204,19 @@
         for dx in x_far:
             index = dx * nz + dz
             push(slot, q_recv.at[dx, dz], qx_s.at[index], qx_r.at[index], (up(x, dx, nx) * nz + z, head))
+
+    load_lists.wait()
+    lists = lists_ref[...].astype(F32)
+    blocks, listed = lists.shape
+    unused = jnp.full((HS - blocks, listed), -1.0, F32)
+    lists = jnp.concatenate([lists, unused, lists, unused], axis=0).T
+    for step in range(ny):
+        for block in range(2):
+            for f in range(2):
+                from_ctx, from_head = frames_from(step, block, f)
+                block_id = ((from_ctx * heads + from_head) * 2 + block).astype(F32)
+                seen = jnp.max(jnp.where(lists == block_id, 1.0, 0.0), axis=0, keepdims=True)
+                bias[step, block, f] = jnp.broadcast_to(jnp.where(seen > 0.0, 0.0, NEG), (8, LANES))
 
     lane = lax.broadcasted_iota(jnp.int32, (1, LANES), 1)
     low = lane < HS
@@ -406,7 +406,7 @@
     heads, group = 2 * ny, nz * own
     rows = nx * group
     keys = ny * 4 * BLK
-    parts = 2 if group >= 4 * HS else 1
+    parts = 1
     each = own // heads
     any_space, vmem = pl.BlockSpec(memory_space=pl.ANY), pl.BlockSpec(memory_space=pltpu.VMEM)
     dma = pltpu.SemaphoreType.DMA

time: 48.5 us -> 48.3 us (level)
  no operation moved by 1% of the time
where the time goes in v6:
time: 48.3 us; the launch traced here: 48.1 us
  Pallas kernels  46.8 us (97%)
  local copies, waits for them, and re-layouts  1.32 us (3%)
    pallas_call x1, Pallas kernels, per_device(): pl.pallas_call(functools.partial(kernel, nx, nz, ny), out_shape=jax.Shape...  46.8 us
    unnamed x1, local copies, waits for them, and re-layouts  1.32 us

profile of v6, /device:TPU:1, one launch (start us, length us, event | category | flops | bytes accessed | tf_op | source)
XLA Modules:
  0.0 48.1 jit_solution(11411465603809703943)
XLA Ops:
  0.0 46.8 %cross_attention.1 = bf16[8,1024]{1,0:T(8,128)(2,1)} custom-call(bf16[64,1024]{1,0:T(8,128)(2,1)} %lat_hbm.1, bf16[256,1024]{1,0:T(8,128)(2,1)} %fr_hbm.1, s32[16,256]{1,0:T(8,128)} %lists_hbm.1, bf16[1024,128]{1,0:T(8,128)(2,1)} %qw_hbm.1, bf16[1024,1024]{1,0:T(8,128)(2,1)} %kw_hbm.1, bf16[1024,1024]{1,0:T(8,128)(2,1)} %vw_hbm.1, bf16[128,1024]{1,0:T(8,128)(2,1)} %ow_hbm.1), custom_call_target="tpu_custom_call" | custom-call | tf_op jit(solution)/shard_map/cross_attention/pallas_call | solution.py:413
  46.8 1.3 %copy.9 = bf16[8,1024]{1,0:T(8,128)(2,1)} copy(bf16[8,1024]{1,0:T(8,128)(2,1)} %cross_attention.1) | data formatting | bytes 32768
